TPU v7x, 32 devices: a whole 2x2x4 slice. The times are simulated.
32 devices in a mesh: groups: 2 (over x), row: 16 (over z, y, core).
Axes of the slice: x: 2, y: 2, z: 4, core: 2. Of those that a mesh axis runs over, the one named last changes fastest.
Arguments:
- pair: bfloat16 [256, 128, 128], P(('groups', 'row')), parts along dimension 0, may hold values from -6 to 6
- single: bfloat16 [256, 384], P(('groups', 'row')), parts along dimension 0, may hold values from -6 to 6
- token_mask: int32 [256], P('groups'), parts along dimension 0, may hold values 0 or 1
- chain_index: int32 [256], P('groups'), parts along dimension 0, may hold values from 0 to 7, as said below
- residue_index: int32 [256], P('groups'), parts along dimension 0, may hold values from 0 to 166, as said below
- pair_gain: float32 [128], replicated, may hold values from 0.25 to 1.75
- pair_norm_offset: float32 [128], replicated, may hold values from -3 to 3
- w_swish_a: bfloat16 [128, 512], replicated, may hold values from -0.5 to 0.5
- w_swish_b: bfloat16 [128, 512], replicated, may hold values from -0.5 to 0.5
- w_trans_out: bfloat16 [512, 128], replicated, may hold values from -0.25 to 0.25
- w_pair_bias: bfloat16 [128, 16], replicated, may hold values from -0.5 to 0.5
- w_project: bfloat16 [384, 1536], replicated, may hold values from -0.3125 to 0.3125
- w_out: bfloat16 [384, 384], replicated, may hold values from -0.3125 to 0.3125
- relative_position_bias: float32 [66, 16], replicated, may hold values from -6 to 300
Outputs:
- new_pair: bfloat16 [256, 128, 128], P(('groups', 'row')), parts along dimension 0
- single_update: bfloat16 [256, 384], P(('groups', 'row')), parts along dimension 0
There are 2 independent parts, one for each index of `groups`. A program takes and returns all parts, laid end to end along the dimension named above; an argument that names none is the same for every part. Nothing has to cross between parts.
Inputs may be any that keep to these rules, and one draw needn't show every extreme that they name: `chain_index`: chain numbers never fall along the tokens, start at 0, and every chain 0 to 7 holds one token or more. `residue_index`: within a chain each token's residue number is one more than the previous token's.
All inputs are finite; a program needn't handle non-finite values.
Results may differ from a plain program's by a relative error of at most 0.014.
Values may be sent and summed in bfloat16 or wider, within the bound.
No kernel may reach another device: no remote copies, remote signals or barrier semaphores. Data moves between devices by JAX's collectives and lax.ppermute only.
A program may use at most 64 MiB of HBM per device.

v0:
```python
import math

import jax
import jax.numpy as jnp
from jax import lax
from jax.sharding import PartitionSpec as P

HEADS = 16
HEAD_DIM = 24
RELMAX = 32
BINS = 66


epsilon = 1e-05


def layer_norm(value_rows):
    middle = jnp.mean(value_rows, axis=-1, keepdims=True)
    centred = value_rows - middle
    spread = jnp.mean(centred * centred, axis=-1, keepdims=True)
    return centred * lax.rsqrt(spread + epsilon)


def relative_bins(res_query, chain_query, res_key, chain_key):
    offset = jnp.clip(res_query[:, None] - res_key[None, :] + RELMAX, 0, 2 * RELMAX)
    return jnp.where(chain_query[:, None] == chain_key[None, :], offset, 2 * RELMAX + 1)


def table_lookup(bins, relative_position_bias):
    classes = jnp.arange(BINS, dtype=jnp.int32)[:, None, None]
    indicator_matrix = (bins[None, :, :] == classes).astype(jnp.float32)
    return jnp.einsum(
        "xzc,xp->pzc", indicator_matrix, relative_position_bias, precision=lax.Precision.HIGHEST
    )


def transition_row(pair_row, pair_gain, pair_norm_offset, w_swish_a, w_swish_b, w_trans_out):
    normed = (layer_norm(pair_row.astype(jnp.float32)) * pair_gain + pair_norm_offset).astype(
        jnp.bfloat16
    )
    first = jnp.dot(normed, w_swish_a, preferred_element_type=jnp.float32)
    second_operand = jnp.dot(normed, w_swish_b, preferred_element_type=jnp.float32)
    hidden = (jax.nn.silu(first) * second_operand).astype(jnp.bfloat16)
    updated = (
        pair_row.astype(jnp.float32)
        + jnp.dot(hidden, w_trans_out, preferred_element_type=jnp.float32)
    ).astype(jnp.bfloat16)
    bias_input = layer_norm(updated.astype(jnp.float32)).astype(jnp.bfloat16)
    return (updated, bias_input)


def on_device(
    pair,
    single,
    token_mask,
    chain_index,
    residue_index,
    pair_gain,
    pair_norm_offset,
    w_swish_a,
    w_swish_b,
    w_trans_out,
    w_pair_bias,
    w_project,
    w_out,
    relative_position_bias,
):
    local_rows = pair.shape[0]
    width = HEADS * HEAD_DIM
    scaling = 1.0 / math.sqrt(HEAD_DIM)
    first_row = lax.axis_index("row") * local_rows

    def one_row(pair_row):
        return transition_row(
            pair_row, pair_gain, pair_norm_offset, w_swish_a, w_swish_b, w_trans_out
        )

    new_pair, bias_input = lax.map(one_row, pair)
    normed = layer_norm(single.astype(jnp.float32)).astype(jnp.bfloat16)
    projected = jnp.dot(normed, w_project, preferred_element_type=jnp.float32).astype(jnp.bfloat16)
    queries = projected[:, :width]
    keys_local = projected[:, width : 2 * width]
    values_local = projected[:, 2 * width : 3 * width]
    gates = projected[:, 3 * width :]
    own_res = lax.dynamic_slice_in_dim(residue_index, first_row, local_rows)
    own_chain = lax.dynamic_slice_in_dim(chain_index, first_row, local_rows)
    extra = table_lookup(
        relative_bins(own_res, own_chain, residue_index, chain_index), relative_position_bias
    )
    extra = jnp.where(token_mask[None, None, :] > 0, extra, -1000000000.0)
    bias_rows = jnp.einsum(
        "rnc,ch->hrn", bias_input, w_pair_bias, preferred_element_type=jnp.float32
    ).astype(jnp.bfloat16)
    own_queries = queries.reshape(local_rows, HEADS, HEAD_DIM)
    top_now = jnp.full((HEADS, local_rows), -1e30, jnp.float32)
    key_piece = lax.all_gather(keys_local, "row", axis=0, tiled=True)
    value_piece = lax.all_gather(values_local, "row", axis=0, tiled=True)
    count = key_piece.shape[0]
    scores = (
        jnp.einsum(
            "rhd,nhd->hrn",
            own_queries,
            key_piece.reshape(count, HEADS, HEAD_DIM),
            preferred_element_type=jnp.float32,
        )
        * scaling
    )
    scores = jnp.where(
        extra > -100000000.0, scores + bias_rows.astype(jnp.float32) + extra, -1000000000.0
    )
    top_next = jnp.maximum(top_now, jnp.max(scores, axis=2))
    expons = jnp.exp(scores - top_next[..., None])
    sum_next = jnp.sum(expons, axis=2)
    acc_next = jnp.einsum(
        "hrn,nhd->hrd",
        expons.astype(jnp.bfloat16),
        value_piece.reshape(count, HEADS, HEAD_DIM),
        preferred_element_type=jnp.float32,
    )
    attended_rows = jnp.transpose(acc_next / sum_next[..., None], (1, 0, 2))
    gated = (
        jax.nn.sigmoid(gates.astype(jnp.float32)) * attended_rows.reshape(local_rows, width)
    ).astype(jnp.bfloat16)
    single_update = jnp.dot(gated, w_out, preferred_element_type=jnp.float32).astype(jnp.bfloat16)
    return (new_pair, single_update)


def solution(mesh):
    return jax.shard_map(
        on_device,
        mesh=mesh,
        in_specs=(
            P(("groups", "row"), None, None),
            P(("groups", "row"), None),
            P("groups"),
            P("groups"),
            P("groups"),
            P(),
            P(),
            P(),
            P(),
            P(),
            P(),
            P(),
            P(),
            P(),
        ),
        out_specs=(P(("groups", "row"), None, None), P(("groups", "row"), None)),
        check_vma=False,
    )
```

profile of v0, /device:TPU:0, one launch (start us, length us, event | category | flops | bytes accessed | tf_op | source)
XLA Modules:
  0.0 81.4 jit_solution(13442811938827215208)
XLA Ops:
  0.7 36.3 %while.12 = (s32[]{:T(128)}, bf16[8,128,128]{2,1,0:T(8,128)(2,1)}, bf16[8,128,128]{1,2,0:T(8,128)(2,1)S(1)}, bf16[8,128,128]{2,1,0:T(8,128)(2,1)}, f32[128]{0:T(...) while((s32[]{:T(128)}, bf16[8,128,128]{2,1,0:T(8,128)(2,1)}, ...), condition=%wide.region_5.6_spmd, body=%wide.region_0.5_spmd.sunk | while | flops 51233024 | bytes 1454201 | solution.py:78
  0.7 0.9 %constant_dynamic-slice_fusion.2 = bf16[1,128,128]{2,1,0:T(8,128)(2,1)S(1)} fusion(bf16[8,128,128]{2,1,0:T(8,128)(2,1)} %get-tuple-element.194, s32[]{:T(128)S(6)} %copy.64), kind=kLoop, calls=%fused_computation.38.clone.1 | loop fusion | bytes 65540 | tf_op jit(solution)/shard_map/while/body/jit(dynamic_index_in_dim)/dynamic_slice | solution.py:78
  1.7 1.2 %fusion.92 = f32[128,512]{1,0:T(8,128)S(1)} fusion(bf16[128,512]{1,0:T(8,128)(2,1)} %get-tuple-element.197, bf16[1,128,128]{1,2,0:T(8,128)(2,1)S(1)} %copy.57, f32[128]{0:T(128)} %get-tuple-element.196, f32[128]{0:T(128)} %get-tuple-element.195, f32[128]{0:T(128)S(1)} %add_rsqrt_fusion.5, f32[128]{0:T(128)S(1)} %broadcast_multiply_fusion.5), kind=kOutput, calls=%fused_computation.26.clone.1 | convolution fusion | flops 16875520 | bytes 428032 | tf_op jit(solution)/shard_map/while/body/eval_jaxpr/dot_general | solution.py:41
  3.0 1.5 %convert_reduce_fusion.6 = (f32[128]{0:T(128)S(1)}, bf16[128,128]{0,1:T(8,128)(2,1)S(1)}) fusion(bf16[512,128]{1,0:T(8,128)(2,1)} %get-tuple-element.199, bf16[128,512]{1,0:T(8,128)(2,1)} %get-tuple-element.198, f32[128,512]{1,0:T(8,128)S(1)} %fusion.92, bf16[1,128,128]{1,2,0:T(8,128)(2,1)S(1)} %copy.57, f32[128]{0:T(128)} %get-tuple-element.196, ...), kind=kOutput, calls=%fused_computation.12.clone.1 | convolution fusion | flops 34127744 | bytes 592384 | tf_op jit(solution)/shard_map/while/body/eval_jaxpr/dot_general | solution.py:46
  4.6 0.6 constant_dynamic-update-slice_fusion.2
  5.3 0.8 constant_dynamic-slice_fusion.2
  6.3 1.2 %fusion.92 = f32[128,512]{1,0:T(8,128)S(1)} fusion(bf16[128,512]{1,0:T(8,128)(2,1)} %get-tuple-element.197, bf16[1,128,128]{1,2,0:T(8,128)(2,1)S(1)} %copy.57, f32[128]{0:T(128)} %get-tuple-element.196, f32[128]{0:T(128)} %get-tuple-element.195, f32[128]{0:T(128)S(1)} %add_rsqrt_fusion.5, f32[128]{0:T(128)S(1)} %broadcast_multiply_fusion.5), kind=kOutput, calls=%fused_computation.26.clone.1 | convolution fusion | flops 16875520 | bytes 428032 | tf_op jit(solution)/shard_map/while/body/eval_jaxpr/dot_general | solution.py:41
  7.5 1.5 %convert_reduce_fusion.6 = (f32[128]{0:T(128)S(1)}, bf16[128,128]{0,1:T(8,128)(2,1)S(1)}) fusion(bf16[512,128]{1,0:T(8,128)(2,1)} %get-tuple-element.199, bf16[128,512]{1,0:T(8,128)(2,1)} %get-tuple-element.198, f32[128,512]{1,0:T(8,128)S(1)} %fusion.92, bf16[1,128,128]{1,2,0:T(8,128)(2,1)S(1)} %copy.57, f32[128]{0:T(128)} %get-tuple-element.196, ...), kind=kOutput, calls=%fused_computation.12.clone.1 | convolution fusion | flops 34127744 | bytes 592384 | tf_op jit(solution)/shard_map/while/body/eval_jaxpr/dot_general | solution.py:46
  9.1 0.6 constant_dynamic-update-slice_fusion.2
  9.8 0.8 constant_dynamic-slice_fusion.2
  10.8 1.2 %fusion.92 = f32[128,512]{1,0:T(8,128)S(1)} fusion(bf16[128,512]{1,0:T(8,128)(2,1)} %get-tuple-element.197, bf16[1,128,128]{1,2,0:T(8,128)(2,1)S(1)} %copy.57, f32[128]{0:T(128)} %get-tuple-element.196, f32[128]{0:T(128)} %get-tuple-element.195, f32[128]{0:T(128)S(1)} %add_rsqrt_fusion.5, f32[128]{0:T(128)S(1)} %broadcast_multiply_fusion.5), kind=kOutput, calls=%fused_computation.26.clone.1 | convolution fusion | flops 16875520 | bytes 428032 | tf_op jit(solution)/shard_map/while/body/eval_jaxpr/dot_general | solution.py:41
  12.1 1.5 %convert_reduce_fusion.6 = (f32[128]{0:T(128)S(1)}, bf16[128,128]{0,1:T(8,128)(2,1)S(1)}) fusion(bf16[512,128]{1,0:T(8,128)(2,1)} %get-tuple-element.199, bf16[128,512]{1,0:T(8,128)(2,1)} %get-tuple-element.198, f32[128,512]{1,0:T(8,128)S(1)} %fusion.92, bf16[1,128,128]{1,2,0:T(8,128)(2,1)S(1)} %copy.57, f32[128]{0:T(128)} %get-tuple-element.196, ...), kind=kOutput, calls=%fused_computation.12.clone.1 | convolution fusion | flops 34127744 | bytes 592384 | tf_op jit(solution)/shard_map/while/body/eval_jaxpr/dot_general | solution.py:46
  13.6 0.6 constant_dynamic-update-slice_fusion.2
  14.4 0.8 constant_dynamic-slice_fusion.2
  15.3 1.2 %fusion.92 = f32[128,512]{1,0:T(8,128)S(1)} fusion(bf16[128,512]{1,0:T(8,128)(2,1)} %get-tuple-element.197, bf16[1,128,128]{1,2,0:T(8,128)(2,1)S(1)} %copy.57, f32[128]{0:T(128)} %get-tuple-element.196, f32[128]{0:T(128)} %get-tuple-element.195, f32[128]{0:T(128)S(1)} %add_rsqrt_fusion.5, f32[128]{0:T(128)S(1)} %broadcast_multiply_fusion.5), kind=kOutput, calls=%fused_computation.26.clone.1 | convolution fusion | flops 16875520 | bytes 428032 | tf_op jit(solution)/shard_map/while/body/eval_jaxpr/dot_general | solution.py:41
  16.6 1.5 %convert_reduce_fusion.6 = (f32[128]{0:T(128)S(1)}, bf16[128,128]{0,1:T(8,128)(2,1)S(1)}) fusion(bf16[512,128]{1,0:T(8,128)(2,1)} %get-tuple-element.199, bf16[128,512]{1,0:T(8,128)(2,1)} %get-tuple-element.198, f32[128,512]{1,0:T(8,128)S(1)} %fusion.92, bf16[1,128,128]{1,2,0:T(8,128)(2,1)S(1)} %copy.57, f32[128]{0:T(128)} %get-tuple-element.196, ...), kind=kOutput, calls=%fused_computation.12.clone.1 | convolution fusion | flops 34127744 | bytes 592384 | tf_op jit(solution)/shard_map/while/body/eval_jaxpr/dot_general | solution.py:46
  18.2 0.6 constant_dynamic-update-slice_fusion.2
  18.9 0.8 constant_dynamic-slice_fusion.2
  19.9 1.2 %fusion.92 = f32[128,512]{1,0:T(8,128)S(1)} fusion(bf16[128,512]{1,0:T(8,128)(2,1)} %get-tuple-element.197, bf16[1,128,128]{1,2,0:T(8,128)(2,1)S(1)} %copy.57, f32[128]{0:T(128)} %get-tuple-element.196, f32[128]{0:T(128)} %get-tuple-element.195, f32[128]{0:T(128)S(1)} %add_rsqrt_fusion.5, f32[128]{0:T(128)S(1)} %broadcast_multiply_fusion.5), kind=kOutput, calls=%fused_computation.26.clone.1 | convolution fusion | flops 16875520 | bytes 428032 | tf_op jit(solution)/shard_map/while/body/eval_jaxpr/dot_general | solution.py:41
  21.1 1.5 %convert_reduce_fusion.6 = (f32[128]{0:T(128)S(1)}, bf16[128,128]{0,1:T(8,128)(2,1)S(1)}) fusion(bf16[512,128]{1,0:T(8,128)(2,1)} %get-tuple-element.199, bf16[128,512]{1,0:T(8,128)(2,1)} %get-tuple-element.198, f32[128,512]{1,0:T(8,128)S(1)} %fusion.92, bf16[1,128,128]{1,2,0:T(8,128)(2,1)S(1)} %copy.57, f32[128]{0:T(128)} %get-tuple-element.196, ...), kind=kOutput, calls=%fused_computation.12.clone.1 | convolution fusion | flops 34127744 | bytes 592384 | tf_op jit(solution)/shard_map/while/body/eval_jaxpr/dot_general | solution.py:46
  23.4 0.8 constant_dynamic-slice_fusion.2
  24.4 1.2 %fusion.92 = f32[128,512]{1,0:T(8,128)S(1)} fusion(bf16[128,512]{1,0:T(8,128)(2,1)} %get-tuple-element.197, bf16[1,128,128]{1,2,0:T(8,128)(2,1)S(1)} %copy.57, f32[128]{0:T(128)} %get-tuple-element.196, f32[128]{0:T(128)} %get-tuple-element.195, f32[128]{0:T(128)S(1)} %add_rsqrt_fusion.5, f32[128]{0:T(128)S(1)} %broadcast_multiply_fusion.5), kind=kOutput, calls=%fused_computation.26.clone.1 | convolution fusion | flops 16875520 | bytes 428032 | tf_op jit(solution)/shard_map/while/body/eval_jaxpr/dot_general | solution.py:41
  25.6 1.5 %convert_reduce_fusion.6 = (f32[128]{0:T(128)S(1)}, bf16[128,128]{0,1:T(8,128)(2,1)S(1)}) fusion(bf16[512,128]{1,0:T(8,128)(2,1)} %get-tuple-element.199, bf16[128,512]{1,0:T(8,128)(2,1)} %get-tuple-element.198, f32[128,512]{1,0:T(8,128)S(1)} %fusion.92, bf16[1,128,128]{1,2,0:T(8,128)(2,1)S(1)} %copy.57, f32[128]{0:T(128)} %get-tuple-element.196, ...), kind=kOutput, calls=%fused_computation.12.clone.1 | convolution fusion | flops 34127744 | bytes 592384 | tf_op jit(solution)/shard_map/while/body/eval_jaxpr/dot_general | solution.py:46
  28.0 0.8 constant_dynamic-slice_fusion.2
  28.9 1.2 %fusion.92 = f32[128,512]{1,0:T(8,128)S(1)} fusion(bf16[128,512]{1,0:T(8,128)(2,1)} %get-tuple-element.197, bf16[1,128,128]{1,2,0:T(8,128)(2,1)S(1)} %copy.57, f32[128]{0:T(128)} %get-tuple-element.196, f32[128]{0:T(128)} %get-tuple-element.195, f32[128]{0:T(128)S(1)} %add_rsqrt_fusion.5, f32[128]{0:T(128)S(1)} %broadcast_multiply_fusion.5), kind=kOutput, calls=%fused_computation.26.clone.1 | convolution fusion | flops 16875520 | bytes 428032 | tf_op jit(solution)/shard_map/while/body/eval_jaxpr/dot_general | solution.py:41
  30.2 1.5 %convert_reduce_fusion.6 = (f32[128]{0:T(128)S(1)}, bf16[128,128]{0,1:T(8,128)(2,1)S(1)}) fusion(bf16[512,128]{1,0:T(8,128)(2,1)} %get-tuple-element.199, bf16[128,512]{1,0:T(8,128)(2,1)} %get-tuple-element.198, f32[128,512]{1,0:T(8,128)S(1)} %fusion.92, bf16[1,128,128]{1,2,0:T(8,128)(2,1)S(1)} %copy.57, f32[128]{0:T(128)} %get-tuple-element.196, ...), kind=kOutput, calls=%fused_computation.12.clone.1 | convolution fusion | flops 34127744 | bytes 592384 | tf_op jit(solution)/shard_map/while/body/eval_jaxpr/dot_general | solution.py:46
  32.5 0.8 constant_dynamic-slice_fusion.2
  33.5 1.2 %fusion.92 = f32[128,512]{1,0:T(8,128)S(1)} fusion(bf16[128,512]{1,0:T(8,128)(2,1)} %get-tuple-element.197, bf16[1,128,128]{1,2,0:T(8,128)(2,1)S(1)} %copy.57, f32[128]{0:T(128)} %get-tuple-element.196, f32[128]{0:T(128)} %get-tuple-element.195, f32[128]{0:T(128)S(1)} %add_rsqrt_fusion.5, f32[128]{0:T(128)S(1)} %broadcast_multiply_fusion.5), kind=kOutput, calls=%fused_computation.26.clone.1 | convolution fusion | flops 16875520 | bytes 428032 | tf_op jit(solution)/shard_map/while/body/eval_jaxpr/dot_general | solution.py:41
  34.7 1.5 %convert_reduce_fusion.6 = (f32[128]{0:T(128)S(1)}, bf16[128,128]{0,1:T(8,128)(2,1)S(1)}) fusion(bf16[512,128]{1,0:T(8,128)(2,1)} %get-tuple-element.199, bf16[128,512]{1,0:T(8,128)(2,1)} %get-tuple-element.198, f32[128,512]{1,0:T(8,128)S(1)} %fusion.92, bf16[1,128,128]{1,2,0:T(8,128)(2,1)S(1)} %copy.57, f32[128]{0:T(128)} %get-tuple-element.196, ...), kind=kOutput, calls=%fused_computation.12.clone.1 | convolution fusion | flops 34127744 | bytes 592384 | tf_op jit(solution)/shard_map/while/body/eval_jaxpr/dot_general | solution.py:46
  37.7 23.5 %all_gather.7 = bf16[128,384]{1,0:T(8,128)(2,1)S(1)} all-gather(bf16[8,384]{1,0:T(8,128)(2,1)S(1)} %get-tuple-element.108), channel_id=1, replica_groups=mesh['groups'=2,'row'=16] {'row'}, dimensions={0}, use_global_device_ids=true | all-gather | bytes 104448 | tf_op jit(solution)/shard_map/all_gather | solution.py:97
  61.8 17.7 %all_gather.6 = bf16[128,384]{1,0:T(8,128)(2,1)S(1)} all-gather(bf16[8,384]{1,0:T(8,128)(2,1)S(1)} %get-tuple-element.109), channel_id=1, replica_groups=mesh['groups'=2,'row'=16] {'row'}, dimensions={0}, use_global_device_ids=true | all-gather | bytes 104448 | tf_op jit(solution)/shard_map/all_gather | solution.py:96
  80.7 0.8 convolution_convert_fusion.2
  (124 shorter events, 7.9 us)
Async XLA Ops:
  0.6 36.8 %copy-start = (bf16[384,1536]{1,0:T(8,128)(2,1)S(1)}, bf16[384,1536]{1,0:T(8,128)(2,1)}, u32[]{:S(2)}) copy-start(bf16[384,1536]{1,0:T(8,128)(2,1)} %param.27) | copy-start | bytes 3538948
  0.7 36.4 %copy-start.2 = (bf16[8,384]{1,0:T(8,128)(2,1)S(1)}, bf16[8,384]{1,0:T(8,128)(2,1)}, u32[]{:S(2)}) copy-start(bf16[8,384]{1,0:T(8,128)(2,1)} %param.17) | copy-start | bytes 18436
  37.0 24.3 %copy-start.4 = (s32[128]{0:T(128)S(1)}, s32[128]{0:T(128)}, u32[]{:S(2)}) copy-start(s32[128]{0:T(128)} %param.20) | copy-start | bytes 1540
  37.0 24.4 %copy-start.5 = (s32[128]{0:T(128)S(1)}, s32[128]{0:T(128)}, u32[]{:S(2)}) copy-start(s32[128]{0:T(128)} %param.19) | copy-start | bytes 1540
  37.0 24.5 %copy-start.7 = (s32[128]{0:T(128)S(1)}, s32[128]{0:T(128)}, u32[]{:S(2)}) copy-start(s32[128]{0:T(128)} %param.18) | copy-start | bytes 1540
  37.0 24.5 %copy-start.6 = (f32[66,16]{0,1:T(8,128)S(1)}, f32[66,16]{0,1:T(8,128)}, u32[]{:S(2)}) copy-start(f32[66,16]{0,1:T(8,128)} %param.29) | copy-start | bytes 12676
  37.1 42.8 %copy-start.3 = (bf16[128,16]{0,1:T(8,128)(2,1)S(1)}, bf16[128,16]{0,1:T(8,128)(2,1)}, u32[]{:S(2)}) copy-start(bf16[128,16]{0,1:T(8,128)(2,1)} %param.26) | copy-start | bytes 12292
  37.7 43.0 %copy-start.1 = (bf16[384,384]{1,0:T(8,128)(2,1)S(1)}, bf16[384,384]{1,0:T(8,128)(2,1)}, u32[]{:S(2)}) copy-start(bf16[384,384]{1,0:T(8,128)(2,1)} %param.28) | copy-start | bytes 884740
where the time goes:
time: 82.4 us; the launch traced here: 81.4 us
  blocking collectives  41.2 us (50%)
  matrix products  23.4 us (28%)
  local copies, waits for them, and re-layouts  13.8 us (17%)
  other arithmetic  1.82 us (2%)
    all_gather x1, blocking collectives, on_device(): value_piece = lax.all_gather(values_local, 'row', axis=0, tiled=True)  23.5 us
    all_gather x1, blocking collectives, on_device(): key_piece = lax.all_gather(keys_local, 'row', axis=0, tiled=True)  17.7 us
    dot_general x8, matrix products, transition_row(): jnp.dot(hidden, w_trans_out, preferred_element_type=jnp.float32)  11.8 us
    dot_general x8, matrix products, transition_row(): first = jnp.dot(normed, w_swish_a, preferred_element_type=jnp.float32)  9.87 us
    dynamic_slice x16, local copies, waits for them, and re-layouts, on_device(): new_pair, bias_input = lax.map(one_row, pair)  7.09 us
    dynamic_update_slice x16, local copies, waits for them, and re-layouts, on_device(): new_pair, bias_input = lax.map(one_row, pair)  5.96 us

commit v1 on v0

v1 whole, which is shorter than its diff:
```python
import functools
import math

import jax
import jax.numpy as jnp
from jax import lax
from jax.experimental import pallas as pl
from jax.experimental.pallas import tpu as pltpu
from jax.sharding import PartitionSpec as P

HEADS = 16
HEAD_DIM = 24
RELMAX = 32
BINS = 66
WIDTH = HEADS * HEAD_DIM
EPSILON = 1e-05
MASKED = -1000000000.0

f32 = jnp.float32
bf16 = jnp.bfloat16
VMEM = pl.BlockSpec(memory_space=pltpu.VMEM)
PARAMS = pltpu.CompilerParams(vmem_limit_bytes=48 * 1024 * 1024)


def layer_norm(rows):
    middle = jnp.mean(rows, axis=-1, keepdims=True)
    centred = rows - middle
    spread = jnp.mean(centred * centred, axis=-1, keepdims=True)
    return centred * lax.rsqrt(spread + EPSILON)


def dot(a, b):
    return jnp.dot(a, b, preferred_element_type=f32)


def dot_nt(a, b):
    return lax.dot_general(a, b, (((1,), (1,)), ((), ())), preferred_element_type=f32)


def head_mask(tokens):
    head = lax.broadcasted_iota(jnp.int32, (tokens, HEADS, WIDTH), 1)
    column = lax.broadcasted_iota(jnp.int32, (tokens, HEADS, WIDTH), 2)
    low = head * HEAD_DIM
    return (column >= low) & (column < low + HEAD_DIM)


def pair_kernel(chunk, pair, gain, shift, w_a, w_b, w_o, w_bias, new_pair, pair_bias):
    rows, tokens, channels = pair.shape
    gains = gain[...][None, :]
    shifts = shift[...][None, :]
    for first in range(0, rows, chunk):
        old = pair[first : first + chunk].reshape(chunk * tokens, channels).astype(f32)
        normed = (layer_norm(old) * gains + shifts).astype(bf16)
        half = dot(normed, w_a[...]) * 0.5
        swish = half + half * jnp.tanh(half)
        hidden = (swish * dot(normed, w_b[...])).astype(bf16)
        updated = (old + dot(hidden, w_o[...])).astype(bf16)
        new_pair[first : first + chunk] = updated.reshape(chunk, tokens, channels)
        bias_input = layer_norm(updated.astype(f32)).astype(bf16)
        for row in range(chunk):
            piece = bias_input[row * tokens : (row + 1) * tokens]
            pair_bias[first + row] = dot_nt(w_bias[...], piece).astype(bf16)


def own_kernel(
    single, w_project, table, chain, residue, mask, pair_bias, queries, gates, added
):
    rows = single.shape[0]
    tokens = chain.shape[0]
    normed = layer_norm(single[...].astype(f32)).astype(bf16)
    query = dot(normed, w_project[:, :WIDTH]).astype(bf16).astype(f32)
    spread = jnp.broadcast_to(query[:, None, :], (rows, HEADS, WIDTH))
    spread = jnp.where(head_mask(rows), spread, 0.0)
    queries[...] = spread.reshape(rows * HEADS, WIDTH).astype(bf16)
    gate = dot(normed, w_project[:, 3 * WIDTH :]).astype(bf16).astype(f32)
    gates[...] = jax.nn.sigmoid(gate)

    first = lax.axis_index("row") * rows
    chain_j = chain[...][None, :]
    residue_j = residue[...][None, :]
    mask_j = mask[...][None, :]
    column = lax.broadcasted_iota(jnp.int32, (rows, tokens), 1)
    own = column == first + lax.broadcasted_iota(jnp.int32, (rows, tokens), 0)
    chain_i = jnp.sum(jnp.where(own, chain_j, 0), axis=1, keepdims=True)
    residue_i = jnp.sum(jnp.where(own, residue_j, 0), axis=1, keepdims=True)
    bins = jnp.clip(residue_i - residue_j + RELMAX, 0, 2 * RELMAX)
    bins = jnp.where(chain_i == chain_j, bins, 2 * RELMAX + 1)
    whole = table[...]
    top = whole.astype(bf16)
    rest = whole - top.astype(f32)
    middle = rest.astype(bf16)
    low = (rest - middle.astype(f32)).astype(bf16)
    pieces = jnp.concatenate([top, middle, low], axis=0)
    classes = lax.broadcasted_iota(jnp.int32, (BINS, tokens), 0)
    for row in range(rows):
        indicator = (classes == bins[row : row + 1]).astype(f32).astype(bf16)
        found = dot(pieces, indicator)
        extra = found[:HEADS] + found[HEADS : 2 * HEADS] + found[2 * HEADS :]
        extra = extra + pair_bias[row].astype(f32)
        added[row] = jnp.where(mask_j > 0, extra, MASKED)


def attend_kernel(
    order, gathered, w_project, queries, gates, added, w_out, update, ordered
):
    rows = gates.shape[0]
    tokens = gathered.shape[0]
    me = lax.axis_index("row")
    arrived = gathered[...].astype(f32)
    for slot, offset in enumerate(order):
        owner = jnp.bitwise_xor(me, offset)
        ordered[pl.ds(pl.multiple_of(owner * rows, rows), rows), :] = arrived[
            slot * rows : (slot + 1) * rows
        ]
    normed = layer_norm(ordered[...]).astype(bf16)
    keys = dot(normed, w_project[:, WIDTH : 2 * WIDTH]).astype(bf16)
    values = dot(normed, w_project[:, 2 * WIDTH : 3 * WIDTH]).astype(bf16)
    extra = added[...].reshape(rows * HEADS, tokens)
    scores = dot_nt(queries[...], keys) * (1.0 / math.sqrt(HEAD_DIM)) + extra
    scores = jnp.where(extra > -100000000.0, scores, MASKED)
    expons = jnp.exp(scores - jnp.max(scores, axis=1, keepdims=True))
    totals = jnp.sum(expons, axis=1, keepdims=True)
    mixed = dot(expons.astype(bf16), values) / totals
    mixed = jnp.where(head_mask(rows), mixed.reshape(rows, HEADS, WIDTH), 0.0)
    gated = (gates[...] * jnp.sum(mixed, axis=1)).astype(bf16)
    update[...] = dot(gated, w_out[...]).astype(bf16)


def gather_rounds(count):
    bits = count.bit_length() - 1
    masks = [(1 << bit) | 1 for bit in range(bits - 1, 0, -1)] + [1]
    if bits < 3:
        return [[m] for m in masks]
    return [[masks[0] ^ masks[1] ^ 1, masks[0], masks[1]]] + [[m] for m in masks[2:]]


def on_device(
    count,
    pair,
    single,
    token_mask,
    chain_index,
    residue_index,
    pair_gain,
    pair_norm_offset,
    w_swish_a,
    w_swish_b,
    w_trans_out,
    w_pair_bias,
    w_project,
    w_out,
    relative_position_bias,
):
    rows, tokens, _ = pair.shape
    width = single.shape[1]
    order = [0]
    gathered = single
    for masks in gather_rounds(count):
        parts = [gathered]
        for mask in masks:
            pairs = [(i, i ^ mask) for i in range(count)]
            parts.append(lax.ppermute(gathered, "row", pairs))
        order = order + [o ^ mask for mask in masks for o in order]
        gathered = jnp.concatenate(parts, axis=0)

    new_pair, pair_bias = pl.pallas_call(
        functools.partial(pair_kernel, max(1, min(rows, 1024 // tokens))),
        out_shape=(
            jax.ShapeDtypeStruct(pair.shape, bf16),
            jax.ShapeDtypeStruct((rows, HEADS, tokens), bf16),
        ),
        in_specs=[VMEM] * 7,
        out_specs=(VMEM, VMEM),
        compiler_params=PARAMS,
        name="pair",
    )(pair, pair_gain, pair_norm_offset, w_swish_a, w_swish_b, w_trans_out, w_pair_bias.T)

    queries, gates, added = pl.pallas_call(
        own_kernel,
        out_shape=(
            jax.ShapeDtypeStruct((rows * HEADS, width), bf16),
            jax.ShapeDtypeStruct((rows, width), f32),
            jax.ShapeDtypeStruct((rows, HEADS, tokens), f32),
        ),
        in_specs=[VMEM] * 7,
        out_specs=(VMEM, VMEM, VMEM),
        compiler_params=PARAMS,
        name="own",
    )(
        single,
        w_project,
        relative_position_bias.T,
        chain_index,
        residue_index,
        token_mask,
        pair_bias,
    )

    update = pl.pallas_call(
        functools.partial(attend_kernel, order),
        out_shape=jax.ShapeDtypeStruct((rows, width), bf16),
        in_specs=[VMEM] * 6,
        out_specs=VMEM,
        scratch_shapes=[pltpu.VMEM((tokens, width), f32)],
        compiler_params=PARAMS,
        name="attend",
    )(gathered, w_project, queries, gates, added, w_out)
    return (new_pair, update)


def solution(mesh):
    return jax.shard_map(
        functools.partial(on_device, mesh.shape["row"]),
        mesh=mesh,
        in_specs=(
            P(("groups", "row"), None, None),
            P(("groups", "row"), None),
            P("groups"),
            P("groups"),
            P("groups"),
            P(),
            P(),
            P(),
            P(),
            P(),
            P(),
            P(),
            P(),
            P(),
        ),
        out_specs=(P(("groups", "row"), None, None), P(("groups", "row"), None)),
        check_vma=False,
    )
```

time: 82.4 us -> 31.3 us (0.38)
  blocking collectives: 41.2 us -> 0 us
  matrix products: 23.4 us -> 0 us
  starting transfers between devices: 0 us -> 6.82 us
  waiting for transfers between devices: 0 us -> 6.34 us
  Pallas kernels: 0 us -> 4.33 us
  local copies, waits for them, and re-layouts: 13.8 us -> 11.9 us
  other arithmetic: 1.82 us -> 0.69 us
    all_gather x2 -> x0, blocking collectives: 41.2 us -> none  [the longest x1 23.5 us: on_device(): value_piece = lax.all_gather(values_local, 'row', axis=0, tiled=True)]
    dot_general x22 -> x0, matrix products: 23.4 us -> none  [the longest x8 11.8 us: transition_row(): jnp.dot(hidden, w_trans_out, preferred_element_type=jnp.float32)]
    unnamed x16 -> x34, local copies, waits for them, and re-layouts: 0.05 us -> 11.9 us
    dynamic_slice x18 -> x0, local copies, waits for them, and re-layouts: 7.24 us -> none  [the longest x16 7.09 us: on_device(): new_pair, bias_input = lax.map(one_row, pair)]
    ppermute x0 -> x5, starting transfers between devices: none -> 6.82 us  [on_device(): parts.append(lax.ppermute(gathered, 'row', pairs))]
    ppermute x0 -> x5, waiting for transfers between devices: none -> 6.34 us  [on_device(): parts.append(lax.ppermute(gathered, 'row', pairs))]
    dynamic_update_slice x16 -> x0, local copies, waits for them, and re-layouts: 5.96 us -> none  [on_device(): new_pair, bias_input = lax.map(one_row, pair)]
    pallas_call x0 -> x3, Pallas kernels: none -> 4.33 us  [the longest x1 2.41 us: on_device(): pl.pallas_call(functools.partial(pair_kernel, max(1, min(rows, 1024 // to...]
  transfers between devices with their start and end apart: 0 -> 5, of which waited for: 0 -> 3; matrix products, arithmetic and copies ran while one was open for 0% -> 3% of each run, Pallas kernels for 0% -> 9%
where the time goes in v1:
time: 31.3 us; the launch traced here: 30.8 us
  local copies, waits for them, and re-layouts  11.9 us (38%)
  starting transfers between devices  6.82 us (22%)
  waiting for transfers between devices  6.34 us (20%)
  Pallas kernels  4.33 us (14%)
  other arithmetic  0.69 us (2%)
  between operations  0.69 us (2%)
    unnamed x34, local copies, waits for them, and re-layouts  11.9 us
    ppermute x5, starting transfers between devices, on_device(): parts.append(lax.ppermute(gathered, 'row', pairs))  6.82 us
    ppermute x5, waiting for transfers between devices, on_device(): parts.append(lax.ppermute(gathered, 'row', pairs))  6.34 us
    pallas_call x1, Pallas kernels, on_device(): pl.pallas_call(functools.partial(pair_kernel, max(1, min(rows, 1024 // to...  2.41 us
    pallas_call x1, Pallas kernels, on_device(): pl.pallas_call(functools.partial(attend_kernel, order), out_shape=jax.Sha...  1.51 us
    concatenate x1, other arithmetic, on_device(): gathered = jnp.concatenate(parts, axis=0)  0.69 us
  transfers between devices with their start and end apart: 5, of which 3 were waited for; matrix products, arithmetic and copies ran while one was open for 3% of the time, Pallas kernels for 9%

profile of v1, /device:TPU:0, one launch (start us, length us, event | category | flops | bytes accessed | tf_op | source)
XLA Modules:
  0.0 30.8 jit_solution(17695222365575598088)
XLA Ops:
  0.6 0.0 copy-start.2
  0.6 2.5 %collective-permute-start.2 = (bf16[8,384]{1,0:T(8,128)(2,1)}, bf16[8,384]{1,0:T(8,128)(2,1)S(1)}, u32[]{:S(2)}, u32[]{:S(2)}) collective-permute-start(bf16[8,384]{1,0:T(8,128)(2,1)} %single.1), channel_id=1, source_target_pairs={{0,5},{1,4},{2,7},{3,6},{4,1},{5,0},{6,3},{7,2},{8,13},{9,12},{10,... | collective-permute-start | bytes 18440 | tf_op jit(solution)/shard_map/ppermute | solution.py:162
  3.2 2.9 %collective-permute-start.1 = (bf16[8,384]{1,0:T(8,128)(2,1)}, bf16[8,384]{1,0:T(8,128)(2,1)S(1)}, u32[]{:S(2)}, u32[]{:S(2)}) collective-permute-start(bf16[8,384]{1,0:T(8,128)(2,1)} %single.1), channel_id=1, source_target_pairs={{0,9},{1,8},{2,11},{3,10},{4,13},{5,12},{6,15},{7,14},{8,1},{9,0},... | collective-permute-start | bytes 18440 | tf_op jit(solution)/shard_map/ppermute | solution.py:162
  6.0 0.0 collective-permute-start
  6.0 0.8 %constant_dynamic-update-slice_fusion.4 = (bf16[64,384]{1,0:T(8,128)(2,1)S(1)}, bf16[128,384]{1,0:T(8,128)(2,1)S(1)}) fusion(bf16[8,384]{1,0:T(8,128)(2,1)} %single.1), kind=kLoop, calls=%fused_computation.5 | loop fusion | bytes 18432
  6.8 0.0 collective-permute-done.2
  6.8 0.8 %collective-permute-done.1 = bf16[8,384]{1,0:T(8,128)(2,1)S(1)} collective-permute-done((bf16[8,384]{1,0:T(8,128)(2,1)}, bf16[8,384]{1,0:T(8,128)(2,1)S(1)}, u32[]{:S(2)}, u32[]{:S(2)}) %collective-permute-start.1) | collective-permute-done | bytes 6176 | tf_op jit(solution)/shard_map/ppermute | solution.py:162
  7.6 3.6 %collective-permute-done = bf16[8,384]{1,0:T(8,128)(2,1)S(1)} collective-permute-done((bf16[8,384]{1,0:T(8,128)(2,1)}, bf16[8,384]{1,0:T(8,128)(2,1)S(1)}, u32[]{:S(2)}, u32[]{:S(2)}) %collective-permute-start) | collective-permute-done | bytes 6176 | tf_op jit(solution)/shard_map/ppermute | solution.py:162
  11.2 0.7 %pad_maximum_fusion = bf16[32,384]{1,0:T(8,128)(2,1)S(1)} fusion(bf16[8,384]{1,0:T(8,128)(2,1)S(1)} %collective-permute-done.2, bf16[8,384]{1,0:T(8,128)(2,1)S(1)} %collective-permute-done.1, bf16[8,384]{1,0:T(8,128)(2,1)S(1)} %collective-permute-done, bf16[8,384]{1,0:T(8,128)(2,1)} %single.1), kind=kLoop, calls=%fused_computation | loop fusion | flops 98304 | bytes 49152 | tf_op jit(solution)/shard_map/concatenate | solution.py:164
  11.8 1.2 %collective-permute-start.3 = (bf16[32,384]{1,0:T(8,128)(2,1)S(1)}, bf16[32,384]{1,0:T(8,128)(2,1)S(1)}, u32[]{:S(2)}, u32[]{:S(2)}) collective-permute-start(bf16[32,384]{1,0:T(8,128)(2,1)S(1)} %pad_maximum_fusion), channel_id=1, source_target_pairs={{0,3},{1,2},{2,1},{3,0},{4,7},{5,6},{6,5},{7,4},{8,11},{9,10},{10,... | collective-permute-start | bytes 73736 | tf_op jit(solution)/shard_map/ppermute | solution.py:162
  13.1 2.0 %collective-permute-done.3 = bf16[32,384]{1,0:T(8,128)(2,1)S(1)} collective-permute-done((bf16[32,384]{1,0:T(8,128)(2,1)S(1)}, bf16[32,384]{1,0:T(8,128)(2,1)S(1)}, u32[]{:S(2)}, u32[]{:S(2)}) %collective-permute-start.3) | collective-permute-done | bytes 24608 | tf_op jit(solution)/shard_map/ppermute | solution.py:162
  15.1 0.2 collective-permute-start.4
  15.3 0.0 copy-start.3
  15.3 0.9 %copy-done.3 = bf16[8,128,128]{2,1,0:T(8,128)(2,1)S(1)} copy-done((bf16[8,128,128]{2,1,0:T(8,128)(2,1)S(1)}, bf16[8,128,128]{2,1,0:T(8,128)(2,1)}, u32[]{:S(2)}) %copy-start.3) | copy-done | bytes 262168
  16.2 0.9 %copy-done.4 = bf16[128,512]{1,0:T(8,128)(2,1)S(1)} copy-done((bf16[128,512]{1,0:T(8,128)(2,1)S(1)}, bf16[128,512]{1,0:T(8,128)(2,1)}, u32[]{:S(2)}) %copy-start.4) | copy-done | bytes 131096
  17.1 0.9 %copy-done.5 = bf16[128,512]{1,0:T(8,128)(2,1)S(1)} copy-done((bf16[128,512]{1,0:T(8,128)(2,1)S(1)}, bf16[128,512]{1,0:T(8,128)(2,1)}, u32[]{:S(2)}) %copy-start.5) | copy-done | bytes 131096
  18.1 0.9 %copy-done.6 = bf16[512,128]{1,0:T(8,128)(2,1)S(1)} copy-done((bf16[512,128]{1,0:T(8,128)(2,1)S(1)}, bf16[512,128]{1,0:T(8,128)(2,1)}, u32[]{:S(2)}) %copy-start.6) | copy-done | bytes 131096
  19.0 0.7 %copy-done.9 = bf16[128,16]{0,1:T(8,128)(2,1)S(1)} copy-done((bf16[128,16]{0,1:T(8,128)(2,1)S(1)}, bf16[128,16]{0,1:T(8,128)(2,1)}, u32[]{:S(2)}) %copy-start.9) | copy-done | bytes 4120
  19.6 0.7 %copy-done.13 = f32[128]{0:T(128)S(1)} copy-done((f32[128]{0:T(128)S(1)}, f32[128]{0:T(128)}, u32[]{:S(2)}) %copy-start.13) | copy-done | bytes 536
  20.3 0.7 %copy-done.14 = f32[128]{0:T(128)S(1)} copy-done((f32[128]{0:T(128)S(1)}, f32[128]{0:T(128)}, u32[]{:S(2)}) %copy-start.14) | copy-done | bytes 536
  21.0 2.4 %pair.2 = (bf16[8,128,128]{2,1,0:T(8,128)(2,1)}, bf16[8,16,128]{2,1,0:T(8,128)(2,1)S(1)}) custom-call(bf16[8,128,128]{2,1,0:T(8,128)(2,1)S(1)} %copy-done.3, f32[128]{0:T(128)S(1)} %copy-done.13, f32[128]{0:T(128)S(1)} %copy-done.14, bf16[128,512]{1,0:T(8,128)(2,1)S(1)} %copy-done.4, bf16[128,512]{1,0:T(8,128)(2,1)S(1)} %copy-done.5, ...), custom_call_target="tpu_custom_call" | custom-call | tf_op jit(solution)/shard_map/pair/pallas_call | solution.py:166
  23.4 1.3 %copy-done = bf16[384,1536]{1,0:T(8,128)(2,1)S(1)} copy-done((bf16[384,1536]{1,0:T(8,128)(2,1)S(1)}, bf16[384,1536]{1,0:T(8,128)(2,1)}, u32[]{:S(2)}) %copy-start) | copy-done | bytes 1179672
  24.6 0.7 %copy-done.7 = bf16[8,384]{1,0:T(8,128)(2,1)S(1)} copy-done((bf16[8,384]{1,0:T(8,128)(2,1)S(1)}, bf16[8,384]{1,0:T(8,128)(2,1)}, u32[]{:S(2)}) %copy-start.7) | copy-done | bytes 6168
  25.3 0.7 %copy-done.8 = f32[66,16]{0,1:T(8,128)S(1)} copy-done((f32[66,16]{0,1:T(8,128)S(1)}, f32[66,16]{0,1:T(8,128)}, u32[]{:S(2)}) %copy-start.8) | copy-done | bytes 4248
  26.0 0.7 %copy-done.10 = s32[128]{0:T(128)S(1)} copy-done((s32[128]{0:T(128)S(1)}, s32[128]{0:T(128)}, u32[]{:S(2)}) %copy-start.10) | copy-done | bytes 536
  26.7 0.7 %copy-done.11 = s32[128]{0:T(128)S(1)} copy-done((s32[128]{0:T(128)S(1)}, s32[128]{0:T(128)}, u32[]{:S(2)}) %copy-start.11) | copy-done | bytes 536
  27.3 0.7 %copy-done.12 = s32[128]{0:T(128)S(1)} copy-done((s32[128]{0:T(128)S(1)}, s32[128]{0:T(128)}, u32[]{:S(2)}) %copy-start.12) | copy-done | bytes 536
  28.0 0.4 %own.1 = (bf16[128,384]{1,0:T(8,128)(2,1)S(1)}, f32[8,384]{1,0:T(8,128)S(1)}, f32[8,16,128]{2,1,0:T(8,128)S(1)}) custom-call(bf16[8,384]{1,0:T(8,128)(2,1)S(1)} %copy-done.7, bf16[384,1536]{1,0:T(8,128)(2,1)S(1)} %copy-done, f32[16,66]{1,0:T(8,128)S(1)} %bitcast.2, s32[128]{0:T(128)S(1)} %copy-done.10, s32[128]{0:T(128)S(1)} %copy-done.11, ...), custom_call_target="tpu_custom_call" | custom-call | tf_op jit(solution)/shard_map/own/pallas_call | solution.py:178
  28.4 0.0 collective-permute-done.4
  28.4 0.0 copy-done.2
  28.4 0.8 %copy-done.1 = bf16[384,1536]{1,0:T(8,128)(2,1)S(1)} copy-done((bf16[384,1536]{1,0:T(8,128)(2,1)S(1)}, bf16[384,1536]{1,0:T(8,128)(2,1)}, u32[]{:S(2)}) %copy-start.1) | copy-done | bytes 1179672
  29.3 1.5 %attend.1 = bf16[8,384]{1,0:T(8,128)(2,1)} custom-call(bf16[128,384]{1,0:T(8,128)(2,1)S(1)} %constant_dynamic-update-slice_fusion.5.gathered, bf16[384,1536]{1,0:T(8,128)(2,1)S(1)} %copy-done.1, bf16[128,384]{1,0:T(8,128)(2,1)S(1)} %get-tuple-element.9.queries, f32[8,384]{1,0:T(8,128)S(1)} %get-tuple-element.10.gates, ...), custom_call_target="tpu_custom_call" | custom-call | tf_op jit(solution)/shard_map/attend/pallas_call | solution.py:199
  (18 shorter events, 0.1 us)
Async XLA Ops:
  0.6 27.8 %copy-start.2 = (bf16[384,384]{1,0:T(8,128)(2,1)S(1)}, bf16[384,384]{1,0:T(8,128)(2,1)}, u32[]{:S(2)}) copy-start(bf16[384,384]{1,0:T(8,128)(2,1)} %w_out.1) | copy-start | bytes 884740
  0.6 6.2 %collective-permute-start.2 = (bf16[8,384]{1,0:T(8,128)(2,1)}, bf16[8,384]{1,0:T(8,128)(2,1)S(1)}, u32[]{:S(2)}, u32[]{:S(2)}) collective-permute-start(bf16[8,384]{1,0:T(8,128)(2,1)} %single.1), channel_id=1, source_target_pairs={{0,5},{1,4},{2,7},{3,6},{4,1},{5,0},{6,3},{7,2},{8,13},{9,12},{10,... | collective-permute-start | bytes 18440 | tf_op jit(solution)/shard_map/ppermute | solution.py:162
  3.2 4.4 %collective-permute-start.1 = (bf16[8,384]{1,0:T(8,128)(2,1)}, bf16[8,384]{1,0:T(8,128)(2,1)S(1)}, u32[]{:S(2)}, u32[]{:S(2)}) collective-permute-start(bf16[8,384]{1,0:T(8,128)(2,1)} %single.1), channel_id=1, source_target_pairs={{0,9},{1,8},{2,11},{3,10},{4,13},{5,12},{6,15},{7,14},{8,1},{9,0},... | collective-permute-start | bytes 18440 | tf_op jit(solution)/shard_map/ppermute | solution.py:162
  6.0 5.1 %collective-permute-start = (bf16[8,384]{1,0:T(8,128)(2,1)}, bf16[8,384]{1,0:T(8,128)(2,1)S(1)}, u32[]{:S(2)}, u32[]{:S(2)}) collective-permute-start(bf16[8,384]{1,0:T(8,128)(2,1)} %single.1), channel_id=1, source_target_pairs={{0,13},{1,12},{2,15},{3,14},{4,9},{5,8},{6,11},{7,10},{8,5},{9,4},... | collective-permute-start | bytes 18440 | tf_op jit(solution)/shard_map/ppermute | solution.py:162
  11.8 3.3 %collective-permute-start.3 = (bf16[32,384]{1,0:T(8,128)(2,1)S(1)}, bf16[32,384]{1,0:T(8,128)(2,1)S(1)}, u32[]{:S(2)}, u32[]{:S(2)}) collective-permute-start(bf16[32,384]{1,0:T(8,128)(2,1)S(1)} %pad_maximum_fusion), channel_id=1, source_target_pairs={{0,3},{1,2},{2,1},{3,0},{4,7},{5,6},{6,5},{7,4},{8,11},{9,10},{10,... | collective-permute-start | bytes 73736 | tf_op jit(solution)/shard_map/ppermute | solution.py:162
  15.1 13.3 %collective-permute-start.4 = (bf16[64,384]{1,0:T(8,128)(2,1)S(1)}, bf16[64,384]{1,0:T(8,128)(2,1)S(1)}, u32[]{:S(2)}, u32[]{:S(2)}) collective-permute-start(bf16[64,384]{1,0:T(8,128)(2,1)S(1)} %get-tuple-element.12), channel_id=1, source_target_pairs={{0,1},{1,0},{2,3},{3,2},{4,5},{5,4},{6,7},{7,6},{8,9},{9,8},{10,11... | collective-permute-start | bytes 147464 | tf_op jit(solution)/shard_map/ppermute | solution.py:162
  15.3 0.9 %copy-start.3 = (bf16[8,128,128]{2,1,0:T(8,128)(2,1)S(1)}, bf16[8,128,128]{2,1,0:T(8,128)(2,1)}, u32[]{:S(2)}) copy-start(bf16[8,128,128]{2,1,0:T(8,128)(2,1)} %pair.3) | copy-start | bytes 786436
  16.2 0.9 %copy-start.4 = (bf16[128,512]{1,0:T(8,128)(2,1)S(1)}, bf16[128,512]{1,0:T(8,128)(2,1)}, u32[]{:S(2)}) copy-start(bf16[128,512]{1,0:T(8,128)(2,1)} %w_a.1) | copy-start | bytes 393220
  17.1 0.9 %copy-start.5 = (bf16[128,512]{1,0:T(8,128)(2,1)S(1)}, bf16[128,512]{1,0:T(8,128)(2,1)}, u32[]{:S(2)}) copy-start(bf16[128,512]{1,0:T(8,128)(2,1)} %w_b.1) | copy-start | bytes 393220
  18.1 0.9 %copy-start.6 = (bf16[512,128]{1,0:T(8,128)(2,1)S(1)}, bf16[512,128]{1,0:T(8,128)(2,1)}, u32[]{:S(2)}) copy-start(bf16[512,128]{1,0:T(8,128)(2,1)} %w_o.1) | copy-start | bytes 393220
  19.0 0.7 %copy-start.9 = (bf16[128,16]{0,1:T(8,128)(2,1)S(1)}, bf16[128,16]{0,1:T(8,128)(2,1)}, u32[]{:S(2)}) copy-start(bf16[128,16]{0,1:T(8,128)(2,1)} %param.24) | copy-start | bytes 12292
  19.6 0.7 %copy-start.13 = (f32[128]{0:T(128)S(1)}, f32[128]{0:T(128)}, u32[]{:S(2)}) copy-start(f32[128]{0:T(128)} %gain.1) | copy-start | bytes 1540
  20.3 0.7 %copy-start.14 = (f32[128]{0:T(128)S(1)}, f32[128]{0:T(128)}, u32[]{:S(2)}) copy-start(f32[128]{0:T(128)} %shift.1) | copy-start | bytes 1540
  23.4 1.3 %copy-start = (bf16[384,1536]{1,0:T(8,128)(2,1)S(1)}, bf16[384,1536]{1,0:T(8,128)(2,1)}, u32[]{:S(2)}) copy-start(bf16[384,1536]{1,0:T(8,128)(2,1)} %w_project.3) | copy-start | bytes 3538948
  24.6 0.7 %copy-start.7 = (bf16[8,384]{1,0:T(8,128)(2,1)S(1)}, bf16[8,384]{1,0:T(8,128)(2,1)}, u32[]{:S(2)}) copy-start(bf16[8,384]{1,0:T(8,128)(2,1)} %single.1) | copy-start | bytes 18436
  25.3 0.7 %copy-start.8 = (f32[66,16]{0,1:T(8,128)S(1)}, f32[66,16]{0,1:T(8,128)}, u32[]{:S(2)}) copy-start(f32[66,16]{0,1:T(8,128)} %param.27) | copy-start | bytes 12676
  26.0 0.7 %copy-start.10 = (s32[128]{0:T(128)S(1)}, s32[128]{0:T(128)}, u32[]{:S(2)}) copy-start(s32[128]{0:T(128)} %chain.1) | copy-start | bytes 1540
  26.7 0.7 %copy-start.11 = (s32[128]{0:T(128)S(1)}, s32[128]{0:T(128)}, u32[]{:S(2)}) copy-start(s32[128]{0:T(128)} %residue.1) | copy-start | bytes 1540
  27.3 0.7 %copy-start.12 = (s32[128]{0:T(128)S(1)}, s32[128]{0:T(128)}, u32[]{:S(2)}) copy-start(s32[128]{0:T(128)} %mask.1) | copy-start | bytes 1540
  28.0 1.3 %copy-start.1 = (bf16[384,1536]{1,0:T(8,128)(2,1)S(1)}, bf16[384,1536]{1,0:T(8,128)(2,1)}, u32[]{:S(2)}) copy-start(bf16[384,1536]{1,0:T(8,128)(2,1)} %w_project.3) | copy-start | bytes 3538948

commit v2 on v1

--- a/solution.py
+++ b/solution.py
@@ -19,6 +19,7 @@
 f32 = jnp.float32
 bf16 = jnp.bfloat16
 VMEM = pl.BlockSpec(memory_space=pltpu.VMEM)
+ANY = pl.BlockSpec(memory_space=pl.ANY)
 PARAMS = pltpu.CompilerParams(vmem_limit_bytes=48 * 1024 * 1024)
 
 
@@ -44,8 +45,25 @@
     return (column >= low) & (column < low + HEAD_DIM)
 
 
-def pair_kernel(chunk, pair, gain, shift, w_a, w_b, w_o, w_bias, new_pair, pair_bias):
+def pair_kernel(chunk, *refs):
+    (pair, gain, shift, w_a, w_b, w_o, w_bias) = refs[:7]
+    later = refs[7:14]
+    new_pair, pair_bias = refs[14:16]
+    kept = refs[16:23]
+    local = refs[23:30]
+    sems = refs[30]
+    sources = (pair, gain, shift, w_a, w_b, w_o, w_bias) + later
+    targets = local + kept
+    copies = [
+        pltpu.make_async_copy(source, target, sems.at[i])
+        for i, (source, target) in enumerate(zip(sources, targets))
+    ]
+    for copy in copies:
+        copy.start()
+    pair, gain, shift, w_a, w_b, w_o, w_bias = local
     rows, tokens, channels = pair.shape
+    for copy in copies[:7]:
+        copy.wait()
     gains = gain[...][None, :]
     shifts = shift[...][None, :]
     for first in range(0, rows, chunk):
@@ -60,11 +78,27 @@
         for row in range(chunk):
             piece = bias_input[row * tokens : (row + 1) * tokens]
             pair_bias[first + row] = dot_nt(w_bias[...], piece).astype(bf16)
+    for copy in copies[7:]:
+        copy.wait()
 
 
 def own_kernel(
-    single, w_project, table, chain, residue, mask, pair_bias, queries, gates, added
+    single,
+    w_project,
+    table,
+    chain,
+    residue,
+    mask,
+    pair_bias,
+    held_pair,
+    queries,
+    gates,
+    added,
+    new_pair,
+    sem,
 ):
+    copy = pltpu.make_async_copy(held_pair, new_pair, sem)
+    copy.start()
     rows = single.shape[0]
     tokens = chain.shape[0]
     normed = layer_norm(single[...].astype(f32)).astype(bf16)
@@ -98,6 +132,7 @@
         extra = found[:HEADS] + found[HEADS : 2 * HEADS] + found[2 * HEADS :]
         extra = extra + pair_bias[row].astype(f32)
         added[row] = jnp.where(mask_j > 0, extra, MASKED)
+    copy.wait()
 
 
 def attend_kernel(
@@ -153,47 +188,72 @@
 ):
     rows, tokens, _ = pair.shape
     width = single.shape[1]
+    operands = (
+        pair,
+        pair_gain,
+        pair_norm_offset,
+        w_swish_a,
+        w_swish_b,
+        w_trans_out,
+        w_pair_bias.T,
+        single,
+        w_project,
+        w_out,
+        relative_position_bias.T,
+        chain_index,
+        residue_index,
+        token_mask,
+    )
+    held = pl.pallas_call(
+        functools.partial(pair_kernel, max(1, min(rows, 1024 // tokens))),
+        out_shape=(
+            jax.ShapeDtypeStruct(pair.shape, bf16),
+            jax.ShapeDtypeStruct((rows, HEADS, tokens), bf16),
+        )
+        + tuple(jax.ShapeDtypeStruct(a.shape, a.dtype) for a in operands[7:]),
+        in_specs=[ANY] * 14,
+        out_specs=(VMEM,) * 9,
+        scratch_shapes=[pltpu.VMEM(a.shape, a.dtype) for a in operands[:7]]
+        + [pltpu.SemaphoreType.DMA((14,))],
+        compiler_params=PARAMS,
+        name="pair",
+    )(*(pltpu.with_memory_space_constraint(a, pltpu.HBM) for a in operands))
+    held_pair, pair_bias, held_single, held_project, held_out = held[:5]
+    held_table, held_chain, held_residue, held_mask = held[5:]
+
     order = [0]
     gathered = single
+    own = held_single
     for masks in gather_rounds(count):
-        parts = [gathered]
+        parts = [own]
         for mask in masks:
             pairs = [(i, i ^ mask) for i in range(count)]
             parts.append(lax.ppermute(gathered, "row", pairs))
         order = order + [o ^ mask for mask in masks for o in order]
-        gathered = jnp.concatenate(parts, axis=0)
-
-    new_pair, pair_bias = pl.pallas_call(
-        functools.partial(pair_kernel, max(1, min(rows, 1024 // tokens))),
-        out_shape=(
-            jax.ShapeDtypeStruct(pair.shape, bf16),
-            jax.ShapeDtypeStruct((rows, HEADS, tokens), bf16),
-        ),
-        in_specs=[VMEM] * 7,
-        out_specs=(VMEM, VMEM),
-        compiler_params=PARAMS,
-        name="pair",
-    )(pair, pair_gain, pair_norm_offset, w_swish_a, w_swish_b, w_trans_out, w_pair_bias.T)
-
-    queries, gates, added = pl.pallas_call(
+        gathered = own = jnp.concatenate(parts, axis=0)
+
+    queries, gates, added, new_pair = pl.pallas_call(
         own_kernel,
         out_shape=(
             jax.ShapeDtypeStruct((rows * HEADS, width), bf16),
             jax.ShapeDtypeStruct((rows, width), f32),
             jax.ShapeDtypeStruct((rows, HEADS, tokens), f32),
+            jax.ShapeDtypeStruct(pair.shape, bf16),
         ),
-        in_specs=[VMEM] * 7,
-        out_specs=(VMEM, VMEM, VMEM),
+        in_specs=[VMEM] * 8,
+        out_specs=(VMEM, VMEM, VMEM, ANY),
+        scratch_shapes=[pltpu.SemaphoreType.DMA],
         compiler_params=PARAMS,
         name="own",
     )(
-        single,
-        w_project,
-        relative_position_bias.T,
-        chain_index,
-        residue_index,
-        token_mask,
+        held_single,
+        held_project,
+        held_table,
+        held_chain,
+        held_residue,
+        held_mask,
         pair_bias,
+        held_pair,
     )
 
     update = pl.pallas_call(
@@ -204,7 +264,7 @@
         scratch_shapes=[pltpu.VMEM((tokens, width), f32)],
         compiler_params=PARAMS,
         name="attend",
-    )(gathered, w_project, queries, gates, added, w_out)
+    )(gathered, held_project, queries, gates, added, held_out)
     return (new_pair, update)
 
 

time: 31.3 us -> 15.9 us (0.51); the launches traced: 30.8 us -> 15.8 us
  local copies, waits for them, and re-layouts: 11.9 us -> 0.05 us
  waiting for transfers between devices: 6.34 us -> 1.77 us
  starting transfers between devices: 6.82 us -> 7.92 us
  Pallas kernels: 4.33 us -> 5.35 us
  other arithmetic: 0.69 us -> 0.01 us
    unnamed x34 -> x4, local copies, waits for them, and re-layouts: 11.9 us -> 0.03 us
    ppermute x5, waiting for transfers between devices: 6.34 us -> 1.77 us  [on_device(): parts.append(lax.ppermute(gathered, 'row', pairs))]
    ppermute x5, starting transfers between devices: 6.82 us -> 7.92 us  [on_device(): parts.append(lax.ppermute(gathered, 'row', pairs))]
    pallas_call x1, Pallas kernels: 2.41 us -> 3.12 us  [on_device(): pl.pallas_call(functools.partial(pair_kernel, max(1, min(rows, 1024 // to...]
    concatenate x1, other arithmetic: 0.69 us -> 0.01 us  [on_device(): gathered = own = jnp.concatenate(parts, axis=0)]
    pallas_call x1, Pallas kernels: 0.41 us -> 0.72 us  [on_device(): pl.pallas_call(own_kernel, out_shape=(jax.ShapeDtypeStruct((rows * HEADS,...]
  transfers between devices with their start and end apart: 5 -> 5, of which waited for: 3 -> 3; matrix products, arithmetic and copies ran while one was open for 3% -> 0% of each run, Pallas kernels for 9% -> 24%
where the time goes in v2:
time: 15.9 us; the launch traced here: 15.8 us
  starting transfers between devices  7.92 us (50%)
  Pallas kernels  5.35 us (34%)
  waiting for transfers between devices  1.77 us (11%)
  between operations  0.67 us (4%)
    ppermute x5, starting transfers between devices, on_device(): parts.append(lax.ppermute(gathered, 'row', pairs))  7.92 us
    pallas_call x1, Pallas kernels, on_device(): pl.pallas_call(functools.partial(pair_kernel, max(1, min(rows, 1024 // to...  3.12 us
    ppermute x5, waiting for transfers between devices, on_device(): parts.append(lax.ppermute(gathered, 'row', pairs))  1.77 us
    pallas_call x1, Pallas kernels, on_device(): pl.pallas_call(functools.partial(attend_kernel, order), out_shape=jax.Sha...  1.52 us
    pallas_call x1, Pallas kernels, on_device(): pl.pallas_call(own_kernel, out_shape=(jax.ShapeDtypeStruct((rows * HEADS,...  0.72 us
  transfers between devices with their start and end apart: 5, of which 3 were waited for; matrix products, arithmetic and copies ran while one was open for 0% of the time, Pallas kernels for 24%

profile of v2, /device:TPU:0, one launch (start us, length us, event | category | flops | bytes accessed | tf_op | source)
XLA Modules:
  0.0 15.8 jit_solution(4796985749870881697)
XLA Ops:
  0.6 4.6 %collective-permute-start = (bf16[8,384]{1,0:T(8,128)(2,1)}, bf16[8,384]{1,0:T(8,128)(2,1)S(1)}, u32[]{:S(2)}, u32[]{:S(2)}) collective-permute-start(bf16[8,384]{1,0:T(8,128)(2,1)} %refs_7_.1), channel_id=1, source_target_pairs={{0,13},{1,12},{2,15},{3,14},{4,9},{5,8},{6,11},{7,10},{8,5},{9,4},... | collective-permute-start | bytes 18440 | tf_op jit(solution)/shard_map/ppermute | solution.py:231
  5.2 0.0 collective-permute-start.1
  5.2 0.9 %collective-permute-start.2 = (bf16[8,384]{1,0:T(8,128)(2,1)}, bf16[8,384]{1,0:T(8,128)(2,1)S(1)}, u32[]{:S(2)}, u32[]{:S(2)}) collective-permute-start(bf16[8,384]{1,0:T(8,128)(2,1)} %refs_7_.1), channel_id=1, source_target_pairs={{0,5},{1,4},{2,7},{3,6},{4,1},{5,0},{6,3},{7,2},{8,13},{9,12},{10,... | collective-permute-start | bytes 18440 | tf_op jit(solution)/shard_map/ppermute | solution.py:231
  6.1 3.1 %pair.1 = (bf16[8,128,128]{2,1,0:T(8,128)(2,1)S(1)}, bf16[8,16,128]{2,1,0:T(8,128)(2,1)S(1)}, bf16[8,384]{1,0:T(8,128)(2,1)S(1)}, bf16[384,1536]{1,0:T(8,128)(2,...) custom-call(bf16[8,128,128]{2,1,0:T(8,128)(2,1)} %refs_0_.1, ...), custom_call_target="tpu_custom_call" | custom-call | tf_op jit(solution)/shard_map/pair/pallas_call | solution.py:207
  9.2 0.0 collective-permute-done
  9.3 0.1 collective-permute-done.1
  9.4 0.0 collective-permute-done.2
  9.4 1.8 %collective-permute-start.3 = (bf16[32,384]{1,0:T(8,128)(2,1)S(1)}, bf16[32,384]{1,0:T(8,128)(2,1)S(1)}, u32[]{:S(2)}, u32[]{:S(2)}) collective-permute-start(bf16[32,384]{1,0:T(8,128)(2,1)S(1)} %pad_maximum_fusion), channel_id=1, source_target_pairs={{0,3},{1,2},{2,1},{3,0},{4,7},{5,6},{6,5},{7,4},{8,11},{9,10},{10,... | collective-permute-start | bytes 73736 | tf_op jit(solution)/shard_map/ppermute | solution.py:231
  11.2 1.5 %collective-permute-done.3 = bf16[32,384]{1,0:T(8,128)(2,1)S(1)} collective-permute-done((bf16[32,384]{1,0:T(8,128)(2,1)S(1)}, bf16[32,384]{1,0:T(8,128)(2,1)S(1)}, u32[]{:S(2)}, u32[]{:S(2)}) %collective-permute-start.3) | collective-permute-done | bytes 24608 | tf_op jit(solution)/shard_map/ppermute | solution.py:231
  12.7 0.7 %collective-permute-start.4 = (bf16[64,384]{1,0:T(8,128)(2,1)S(1)}, bf16[64,384]{1,0:T(8,128)(2,1)S(1)}, u32[]{:S(2)}, u32[]{:S(2)}) collective-permute-start(bf16[64,384]{1,0:T(8,128)(2,1)S(1)} %get-tuple-element.28), channel_id=1, source_target_pairs={{0,1},{1,0},{2,3},{3,2},{4,5},{5,4},{6,7},{7,6},{8,9},{9,8},{10,11... | collective-permute-start | bytes 147464 | tf_op jit(solution)/shard_map/ppermute | solution.py:231
  13.4 0.7 %own.1 = (bf16[128,384]{1,0:T(8,128)(2,1)S(1)}, f32[8,384]{1,0:T(8,128)S(1)}, f32[8,16,128]{2,1,0:T(8,128)S(1)}, bf16[8,128,128]{2,1,0:T(8,128)(2,1)}) custom-call(bf16[8,384]{1,0:T(8,128)(2,1)S(1)} %get-tuple-element.15.single, bf16[384,1536]{1,0:T(8,128)(2,1)S(1)} %get-tuple-element.16.w_project, f32[16,66]{1,0:T(8,128)S(1)} %get-tuple-element.17.table, ...), custom_call_target="tpu_custom_call" | custom-call | tf_op jit(solution)/shard_map/own/pallas_call | solution.py:235
  14.1 0.2 collective-permute-done.4
  14.3 1.5 %attend.1 = bf16[8,384]{1,0:T(8,128)(2,1)} custom-call(bf16[128,384]{1,0:T(8,128)(2,1)S(1)} %constant_dynamic-update-slice_fusion.5.gathered, bf16[384,1536]{1,0:T(8,128)(2,1)S(1)} %get-tuple-element.16.w_project, bf16[128,384]{1,0:T(8,128)(2,1)S(1)} %get-tuple-element.24.queries, f32[8,384]{1,0:T(8,128)S(1)} %get-tuple-element.25.gates, ...), custom_call_target="tpu_custom_call" | custom-call | tf_op jit(solution)/shard_map/attend/pallas_call | solution.py:259
  (7 shorter events, 0.1 us)
Async XLA Ops:
  0.6 8.6 %collective-permute-start = (bf16[8,384]{1,0:T(8,128)(2,1)}, bf16[8,384]{1,0:T(8,128)(2,1)S(1)}, u32[]{:S(2)}, u32[]{:S(2)}) collective-permute-start(bf16[8,384]{1,0:T(8,128)(2,1)} %refs_7_.1), channel_id=1, source_target_pairs={{0,13},{1,12},{2,15},{3,14},{4,9},{5,8},{6,11},{7,10},{8,5},{9,4},... | collective-permute-start | bytes 18440 | tf_op jit(solution)/shard_map/ppermute | solution.py:231
  5.2 4.2 %collective-permute-start.1 = (bf16[8,384]{1,0:T(8,128)(2,1)}, bf16[8,384]{1,0:T(8,128)(2,1)S(1)}, u32[]{:S(2)}, u32[]{:S(2)}) collective-permute-start(bf16[8,384]{1,0:T(8,128)(2,1)} %refs_7_.1), channel_id=1, source_target_pairs={{0,9},{1,8},{2,11},{3,10},{4,13},{5,12},{6,15},{7,14},{8,1},{9,0},... | collective-permute-start | bytes 18440 | tf_op jit(solution)/shard_map/ppermute | solution.py:231
  5.2 4.2 %collective-permute-start.2 = (bf16[8,384]{1,0:T(8,128)(2,1)}, bf16[8,384]{1,0:T(8,128)(2,1)S(1)}, u32[]{:S(2)}, u32[]{:S(2)}) collective-permute-start(bf16[8,384]{1,0:T(8,128)(2,1)} %refs_7_.1), channel_id=1, source_target_pairs={{0,5},{1,4},{2,7},{3,6},{4,1},{5,0},{6,3},{7,2},{8,13},{9,12},{10,... | collective-permute-start | bytes 18440 | tf_op jit(solution)/shard_map/ppermute | solution.py:231
  9.4 3.3 %collective-permute-start.3 = (bf16[32,384]{1,0:T(8,128)(2,1)S(1)}, bf16[32,384]{1,0:T(8,128)(2,1)S(1)}, u32[]{:S(2)}, u32[]{:S(2)}) collective-permute-start(bf16[32,384]{1,0:T(8,128)(2,1)S(1)} %pad_maximum_fusion), channel_id=1, source_target_pairs={{0,3},{1,2},{2,1},{3,0},{4,7},{5,6},{6,5},{7,4},{8,11},{9,10},{10,... | collective-permute-start | bytes 73736 | tf_op jit(solution)/shard_map/ppermute | solution.py:231
  12.7 1.6 %collective-permute-start.4 = (bf16[64,384]{1,0:T(8,128)(2,1)S(1)}, bf16[64,384]{1,0:T(8,128)(2,1)S(1)}, u32[]{:S(2)}, u32[]{:S(2)}) collective-permute-start(bf16[64,384]{1,0:T(8,128)(2,1)S(1)} %get-tuple-element.28), channel_id=1, source_target_pairs={{0,1},{1,0},{2,3},{3,2},{4,5},{5,4},{6,7},{7,6},{8,9},{9,8},{10,11... | collective-permute-start | bytes 147464 | tf_op jit(solution)/shard_map/ppermute | solution.py:231

commit v3 on v2

--- a/solution.py
+++ b/solution.py
@@ -15,6 +15,7 @@
 WIDTH = HEADS * HEAD_DIM
 EPSILON = 1e-05
 MASKED = -1000000000.0
+EARLY = 6
 
 f32 = jnp.float32
 bf16 = jnp.bfloat16
@@ -45,25 +46,9 @@
     return (column >= low) & (column < low + HEAD_DIM)
 
 
-def pair_kernel(chunk, *refs):
-    (pair, gain, shift, w_a, w_b, w_o, w_bias) = refs[:7]
-    later = refs[7:14]
-    new_pair, pair_bias = refs[14:16]
-    kept = refs[16:23]
-    local = refs[23:30]
-    sems = refs[30]
-    sources = (pair, gain, shift, w_a, w_b, w_o, w_bias) + later
-    targets = local + kept
-    copies = [
-        pltpu.make_async_copy(source, target, sems.at[i])
-        for i, (source, target) in enumerate(zip(sources, targets))
-    ]
-    for copy in copies:
-        copy.start()
-    pair, gain, shift, w_a, w_b, w_o, w_bias = local
+def transition(pair, weights, chunk, new_pair, pair_bias, first_bias):
+    gain, shift, w_a, w_b, w_o, w_bias = weights
     rows, tokens, channels = pair.shape
-    for copy in copies[:7]:
-        copy.wait()
     gains = gain[...][None, :]
     shifts = shift[...][None, :]
     for first in range(0, rows, chunk):
@@ -77,28 +62,46 @@
         bias_input = layer_norm(updated.astype(f32)).astype(bf16)
         for row in range(chunk):
             piece = bias_input[row * tokens : (row + 1) * tokens]
-            pair_bias[first + row] = dot_nt(w_bias[...], piece).astype(bf16)
+            pair_bias[first_bias + first + row] = dot_nt(w_bias[...], piece).astype(bf16)
+
+
+def early_kernel(early, chunk, *refs):
+    sources = refs[:14]
+    new_pair, pair_bias, late_pair = refs[14:17]
+    kept = refs[17:30]
+    early_pair, sems = refs[30:]
+    rows = sources[0].shape[0]
+    starts = [
+        (sources[0].at[pl.ds(0, early)], early_pair),
+        *zip(sources[1:7], kept[:6]),
+        (sources[0].at[pl.ds(early, rows - early)], late_pair),
+        *zip(sources[7:], kept[6:]),
+    ]
+    copies = [pltpu.make_async_copy(*ends, sems.at[i]) for i, ends in enumerate(starts)]
+    for copy in copies:
+        copy.start()
+    for copy in copies[:7]:
+        copy.wait()
+    transition(early_pair, kept[:6], chunk, new_pair, pair_bias, 0)
     for copy in copies[7:]:
         copy.wait()
 
 
-def own_kernel(
-    single,
-    w_project,
-    table,
-    chain,
-    residue,
-    mask,
-    pair_bias,
-    held_pair,
-    queries,
-    gates,
-    added,
-    new_pair,
-    sem,
-):
-    copy = pltpu.make_async_copy(held_pair, new_pair, sem)
+def late_kernel(chunk, *refs):
+    weights = refs[:6]
+    single, w_project, table, chain, residue, mask = refs[6:12]
+    early_pair, early_bias, late_pair, received = refs[12:16]
+    queries, gates, added, new_pair, passed = refs[16:21]
+    late_new, late_bias, sems = refs[21:]
+    early = early_pair.shape[0]
+    late = late_pair.shape[0]
+    first_copy = pltpu.make_async_copy(early_pair, new_pair.at[pl.ds(0, early)], sems.at[0])
+    first_copy.start()
+    passed[...] = received[...]
+    transition(late_pair, weights, chunk, late_new, late_bias, 0)
+    copy = pltpu.make_async_copy(late_new, new_pair.at[pl.ds(early, late)], sems.at[1])
     copy.start()
+
     rows = single.shape[0]
     tokens = chain.shape[0]
     normed = layer_norm(single[...].astype(f32)).astype(bf16)
@@ -130,8 +133,10 @@
         indicator = (classes == bins[row : row + 1]).astype(f32).astype(bf16)
         found = dot(pieces, indicator)
         extra = found[:HEADS] + found[HEADS : 2 * HEADS] + found[2 * HEADS :]
-        extra = extra + pair_bias[row].astype(f32)
+        bias = early_bias[row] if row < early else late_bias[row - early]
+        extra = extra + bias.astype(f32)
         added[row] = jnp.where(mask_j > 0, extra, MASKED)
+    first_copy.wait()
     copy.wait()
 
 
@@ -161,12 +166,16 @@
     update[...] = dot(gated, w_out[...]).astype(bf16)
 
 
+def chunk_of(rows, tokens):
+    return max(d for d in range(1, rows + 1) if rows % d == 0 and (d == 1 or d * tokens <= 1024))
+
+
 def gather_rounds(count):
     bits = count.bit_length() - 1
     masks = [(1 << bit) | 1 for bit in range(bits - 1, 0, -1)] + [1]
     if bits < 3:
         return [[m] for m in masks]
-    return [[masks[0] ^ masks[1] ^ 1, masks[0], masks[1]]] + [[m] for m in masks[2:]]
+    return [[masks[0], masks[1], masks[0] ^ masks[1] ^ 1]] + [[m] for m in masks[2:]]
 
 
 def on_device(
@@ -204,57 +213,69 @@
         residue_index,
         token_mask,
     )
+    early = max(1, EARLY * rows // 8)
+    late = rows - early
     held = pl.pallas_call(
-        functools.partial(pair_kernel, max(1, min(rows, 1024 // tokens))),
+        functools.partial(early_kernel, early, chunk_of(early, tokens)),
         out_shape=(
-            jax.ShapeDtypeStruct(pair.shape, bf16),
-            jax.ShapeDtypeStruct((rows, HEADS, tokens), bf16),
+            jax.ShapeDtypeStruct((early,) + pair.shape[1:], bf16),
+            jax.ShapeDtypeStruct((early, HEADS, tokens), bf16),
+            jax.ShapeDtypeStruct((late,) + pair.shape[1:], bf16),
         )
-        + tuple(jax.ShapeDtypeStruct(a.shape, a.dtype) for a in operands[7:]),
+        + tuple(jax.ShapeDtypeStruct(a.shape, a.dtype) for a in operands[1:]),
         in_specs=[ANY] * 14,
-        out_specs=(VMEM,) * 9,
-        scratch_shapes=[pltpu.VMEM(a.shape, a.dtype) for a in operands[:7]]
-        + [pltpu.SemaphoreType.DMA((14,))],
+        out_specs=(VMEM,) * 16,
+        scratch_shapes=[
+            pltpu.VMEM((early,) + pair.shape[1:], bf16),
+            pltpu.SemaphoreType.DMA((15,)),
+        ],
         compiler_params=PARAMS,
-        name="pair",
+        name="early",
     )(*(pltpu.with_memory_space_constraint(a, pltpu.HBM) for a in operands))
-    held_pair, pair_bias, held_single, held_project, held_out = held[:5]
-    held_table, held_chain, held_residue, held_mask = held[5:]
+    early_pair, early_bias, late_pair = held[:3]
+    weights = held[3:9]
+    held_single, held_project, held_out = held[9:12]
+    places = held[12:16]
 
     order = [0]
     gathered = single
     own = held_single
-    for masks in gather_rounds(count):
+    for step, masks in enumerate(gather_rounds(count)):
         parts = [own]
         for mask in masks:
             pairs = [(i, i ^ mask) for i in range(count)]
             parts.append(lax.ppermute(gathered, "row", pairs))
+        if step == 1:
+            queries, gates, added, new_pair, parts[0] = pl.pallas_call(
+                functools.partial(late_kernel, chunk_of(late, tokens)),
+                out_shape=(
+                    jax.ShapeDtypeStruct((rows * HEADS, width), bf16),
+                    jax.ShapeDtypeStruct((rows, width), f32),
+                    jax.ShapeDtypeStruct((rows, HEADS, tokens), f32),
+                    jax.ShapeDtypeStruct(pair.shape, bf16),
+                    jax.ShapeDtypeStruct(own.shape, own.dtype),
+                ),
+                in_specs=[VMEM] * 16,
+                out_specs=(VMEM, VMEM, VMEM, ANY, VMEM),
+                scratch_shapes=[
+                    pltpu.VMEM((late,) + pair.shape[1:], bf16),
+                    pltpu.VMEM((late, HEADS, tokens), bf16),
+                    pltpu.SemaphoreType.DMA((2,)),
+                ],
+                compiler_params=PARAMS,
+                name="late",
+            )(
+                *weights,
+                held_single,
+                held_project,
+                *places,
+                early_pair,
+                early_bias,
+                late_pair,
+                own,
+            )
         order = order + [o ^ mask for mask in masks for o in order]
         gathered = own = jnp.concatenate(parts, axis=0)
-
-    queries, gates, added, new_pair = pl.pallas_call(
-        own_kernel,
-        out_shape=(
-            jax.ShapeDtypeStruct((rows * HEADS, width), bf16),
-            jax.ShapeDtypeStruct((rows, width), f32),
-            jax.ShapeDtypeStruct((rows, HEADS, tokens), f32),
-            jax.ShapeDtypeStruct(pair.shape, bf16),
-        ),
-        in_specs=[VMEM] * 8,
-        out_specs=(VMEM, VMEM, VMEM, ANY),
-        scratch_shapes=[pltpu.SemaphoreType.DMA],
-        compiler_params=PARAMS,
-        name="own",
-    )(
-        held_single,
-        held_project,
-        held_table,
-        held_chain,
-        held_residue,
-        held_mask,
-        pair_bias,
-        held_pair,
-    )
 
     update = pl.pallas_call(
         functools.partial(attend_kernel, order),

time: 15.9 us -> 15.7 us (0.987)
  waiting for transfers between devices: 1.77 us -> 1.33 us
  Pallas kernels: 5.35 us -> 5.73 us
    ppermute x5, waiting for transfers between devices: 1.77 us -> 1.33 us  [on_device(): parts.append(lax.ppermute(gathered, 'row', pairs))]
    pallas_call x2, Pallas kernels: 3.84 us -> 4.22 us  [the longest x1 2.81 us: on_device(): pl.pallas_call(functools.partial(early_kernel, early, chunk_of(early, tok...]
  transfers between devices with their start and end apart: 5 -> 5, of which waited for: 3 -> 4; matrix products, arithmetic and copies ran while one was open for 0% -> 0% of each run, Pallas kernels for 24% -> 27%
where the time goes in v3:
time: 15.7 us; the launch traced here: 15.6 us
  starting transfers between devices  7.81 us (50%)
  Pallas kernels  5.73 us (36%)
  waiting for transfers between devices  1.33 us (8%)
  between operations  0.68 us (4%)
    ppermute x5, starting transfers between devices, on_device(): parts.append(lax.ppermute(gathered, 'row', pairs))  7.81 us
    pallas_call x1, Pallas kernels, on_device(): pl.pallas_call(functools.partial(early_kernel, early, chunk_of(early, tok...  2.81 us
    pallas_call x1, Pallas kernels, on_device(): pl.pallas_call(functools.partial(attend_kernel, order), out_shape=jax.Sha...  1.52 us
    pallas_call x1, Pallas kernels, on_device(): pl.pallas_call(functools.partial(late_kernel, chunk_of(late, tokens)), ou...  1.41 us
    ppermute x5, waiting for transfers between devices, on_device(): parts.append(lax.ppermute(gathered, 'row', pairs))  1.33 us
  transfers between devices with their start and end apart: 5, of which 4 were waited for; matrix products, arithmetic and copies ran while one was open for 0% of the time, Pallas kernels for 27%

profile of v3, /device:TPU:0, one launch (start us, length us, event | category | flops | bytes accessed | tf_op | source)
XLA Modules:
  0.0 15.6 jit_solution(10717224496457462938)
XLA Ops:
  0.6 3.5 %collective-permute-start = (bf16[8,384]{1,0:T(8,128)(2,1)}, bf16[8,384]{1,0:T(8,128)(2,1)S(1)}, u32[]{:S(2)}, u32[]{:S(2)}) collective-permute-start(bf16[8,384]{1,0:T(8,128)(2,1)} %refs_7_.1), channel_id=1, source_target_pairs={{0,9},{1,8},{2,11},{3,10},{4,13},{5,12},{6,15},{7,14},{8,1},{9,0},... | collective-permute-start | bytes 18440 | tf_op jit(solution)/shard_map/ppermute | solution.py:247
  4.2 1.6 %collective-permute-start.2 = (bf16[8,384]{1,0:T(8,128)(2,1)}, bf16[8,384]{1,0:T(8,128)(2,1)S(1)}, u32[]{:S(2)}, u32[]{:S(2)}) collective-permute-start(bf16[8,384]{1,0:T(8,128)(2,1)} %refs_7_.1), channel_id=1, source_target_pairs={{0,13},{1,12},{2,15},{3,14},{4,9},{5,8},{6,11},{7,10},{8,5},{9,4},... | collective-permute-start | bytes 18440 | tf_op jit(solution)/shard_map/ppermute | solution.py:247
  5.8 0.2 %collective-permute-start.1 = (bf16[8,384]{1,0:T(8,128)(2,1)}, bf16[8,384]{1,0:T(8,128)(2,1)S(1)}, u32[]{:S(2)}, u32[]{:S(2)}) collective-permute-start(bf16[8,384]{1,0:T(8,128)(2,1)} %refs_7_.1), channel_id=1, source_target_pairs={{0,5},{1,4},{2,7},{3,6},{4,1},{5,0},{6,3},{7,2},{8,13},{9,12},{10,... | collective-permute-start | bytes 18440 | tf_op jit(solution)/shard_map/ppermute | solution.py:247
  6.0 2.8 %early.1 = (bf16[6,128,128]{2,1,0:T(8,128)(2,1)S(1)}, bf16[6,16,128]{2,1,0:T(8,128)(2,1)S(1)}, bf16[2,128,128]{2,1,0:T(8,128)(2,1)S(1)}, f32[128]{0:T(128)S(1)},...) custom-call(bf16[8,128,128]{2,1,0:T(8,128)(2,1)} %refs_0_.1, ...), custom_call_target="tpu_custom_call" | custom-call | tf_op jit(solution)/shard_map/early/pallas_call | solution.py:218
  8.9 0.0 collective-permute-done
  8.9 0.2 %collective-permute-done.1 = bf16[8,384]{1,0:T(8,128)(2,1)S(1)} collective-permute-done((bf16[8,384]{1,0:T(8,128)(2,1)}, bf16[8,384]{1,0:T(8,128)(2,1)S(1)}, u32[]{:S(2)}, u32[]{:S(2)}) %collective-permute-start.1) | collective-permute-done | bytes 6176 | tf_op jit(solution)/shard_map/ppermute | solution.py:247
  9.1 0.2 %collective-permute-done.2 = bf16[8,384]{1,0:T(8,128)(2,1)S(1)} collective-permute-done((bf16[8,384]{1,0:T(8,128)(2,1)}, bf16[8,384]{1,0:T(8,128)(2,1)S(1)}, u32[]{:S(2)}, u32[]{:S(2)}) %collective-permute-start.2) | collective-permute-done | bytes 6176 | tf_op jit(solution)/shard_map/ppermute | solution.py:247
  9.2 1.8 %collective-permute-start.3 = (bf16[32,384]{1,0:T(8,128)(2,1)S(1)}, bf16[32,384]{1,0:T(8,128)(2,1)S(1)}, u32[]{:S(2)}, u32[]{:S(2)}) collective-permute-start(bf16[32,384]{1,0:T(8,128)(2,1)S(1)} %constant_dynamic-update-slice_fusion.refs_15_), channel_id=1, source_target_pairs={{0,3},{1,2},{2,1},{3,0},{4,7},{5,6},{6,5},{7,4},{8,11},{9,10},{10,... | collective-permute-start | bytes 73736 | tf_op jit(solution)/shard_map/ppermute | solution.py:247
  11.0 1.4 %late.1 = (bf16[128,384]{1,0:T(8,128)(2,1)S(1)}, f32[8,384]{1,0:T(8,128)S(1)}, f32[8,16,128]{2,1,0:T(8,128)S(1)}, bf16[8,128,128]{2,1,0:T(8,128)(2,1)}, bf16[32,384]{1,0:T(8,128)(2,1)S(1)}) custom-call(f32[128]{0:T(128)S(1)} %get-tuple-element.23.refs_0_, f32[128]{0:T(128)S(1)} %get-tuple-element.24.refs_1_, bf16[128,512]{1,0:T(8,128)(2,1)S(1)} %get-tuple-element.25.refs_2_, ...), custom_call_target="tpu_custom_call" | custom-call | tf_op jit(solution)/shard_map/late/pallas_call | solution.py:249
  12.5 0.1 collective-permute-done.3
  12.6 0.6 %collective-permute-start.4 = (bf16[64,384]{1,0:T(8,128)(2,1)S(1)}, bf16[64,384]{1,0:T(8,128)(2,1)S(1)}, u32[]{:S(2)}, u32[]{:S(2)}) collective-permute-start(bf16[64,384]{1,0:T(8,128)(2,1)S(1)} %pad_maximum_fusion.1), channel_id=1, source_target_pairs={{0,1},{1,0},{2,3},{3,2},{4,5},{5,4},{6,7},{7,6},{8,9},{9,8},{10,11... | collective-permute-start | bytes 147464 | tf_op jit(solution)/shard_map/ppermute | solution.py:247
  13.2 0.9 %collective-permute-done.4 = bf16[64,384]{1,0:T(8,128)(2,1)S(1)} collective-permute-done((bf16[64,384]{1,0:T(8,128)(2,1)S(1)}, bf16[64,384]{1,0:T(8,128)(2,1)S(1)}, u32[]{:S(2)}, u32[]{:S(2)}) %collective-permute-start.4) | collective-permute-done | bytes 49184 | tf_op jit(solution)/shard_map/ppermute | solution.py:247
  14.1 1.5 %attend.1 = bf16[8,384]{1,0:T(8,128)(2,1)} custom-call(bf16[128,384]{1,0:T(8,128)(2,1)S(1)} %pad_maximum_fusion.gathered, bf16[384,1536]{1,0:T(8,128)(2,1)S(1)} %get-tuple-element.30.refs_7_.w_project, bf16[128,384]{1,0:T(8,128)(2,1)S(1)} %get-tuple-element.40.queries, f32[8,384]{1,0:T(8,128)S(1)} %get-tuple-element.41.gates, ...), custom_call_target="tpu_custom_call" | custom-call | tf_op jit(solution)/shard_map/attend/pallas_call | solution.py:280
  (6 shorter events, 0.0 us)
Async XLA Ops:
  0.6 8.2 %collective-permute-start = (bf16[8,384]{1,0:T(8,128)(2,1)}, bf16[8,384]{1,0:T(8,128)(2,1)S(1)}, u32[]{:S(2)}, u32[]{:S(2)}) collective-permute-start(bf16[8,384]{1,0:T(8,128)(2,1)} %refs_7_.1), channel_id=1, source_target_pairs={{0,9},{1,8},{2,11},{3,10},{4,13},{5,12},{6,15},{7,14},{8,1},{9,0},... | collective-permute-start | bytes 18440 | tf_op jit(solution)/shard_map/ppermute | solution.py:247
  4.2 5.1 %collective-permute-start.2 = (bf16[8,384]{1,0:T(8,128)(2,1)}, bf16[8,384]{1,0:T(8,128)(2,1)S(1)}, u32[]{:S(2)}, u32[]{:S(2)}) collective-permute-start(bf16[8,384]{1,0:T(8,128)(2,1)} %refs_7_.1), channel_id=1, source_target_pairs={{0,13},{1,12},{2,15},{3,14},{4,9},{5,8},{6,11},{7,10},{8,5},{9,4},... | collective-permute-start | bytes 18440 | tf_op jit(solution)/shard_map/ppermute | solution.py:247
  5.8 3.3 %collective-permute-start.1 = (bf16[8,384]{1,0:T(8,128)(2,1)}, bf16[8,384]{1,0:T(8,128)(2,1)S(1)}, u32[]{:S(2)}, u32[]{:S(2)}) collective-permute-start(bf16[8,384]{1,0:T(8,128)(2,1)} %refs_7_.1), channel_id=1, source_target_pairs={{0,5},{1,4},{2,7},{3,6},{4,1},{5,0},{6,3},{7,2},{8,13},{9,12},{10,... | collective-permute-start | bytes 18440 | tf_op jit(solution)/shard_map/ppermute | solution.py:247
  9.2 3.3 %collective-permute-start.3 = (bf16[32,384]{1,0:T(8,128)(2,1)S(1)}, bf16[32,384]{1,0:T(8,128)(2,1)S(1)}, u32[]{:S(2)}, u32[]{:S(2)}) collective-permute-start(bf16[32,384]{1,0:T(8,128)(2,1)S(1)} %constant_dynamic-update-slice_fusion.refs_15_), channel_id=1, source_target_pairs={{0,3},{1,2},{2,1},{3,0},{4,7},{5,6},{6,5},{7,4},{8,11},{9,10},{10,... | collective-permute-start | bytes 73736 | tf_op jit(solution)/shard_map/ppermute | solution.py:247
  12.6 1.5 %collective-permute-start.4 = (bf16[64,384]{1,0:T(8,128)(2,1)S(1)}, bf16[64,384]{1,0:T(8,128)(2,1)S(1)}, u32[]{:S(2)}, u32[]{:S(2)}) collective-permute-start(bf16[64,384]{1,0:T(8,128)(2,1)S(1)} %pad_maximum_fusion.1), channel_id=1, source_target_pairs={{0,1},{1,0},{2,3},{3,2},{4,5},{5,4},{6,7},{7,6},{8,9},{9,8},{10,11... | collective-permute-start | bytes 147464 | tf_op jit(solution)/shard_map/ppermute | solution.py:247

commit v4 on v3

--- a/solution.py
+++ b/solution.py
@@ -147,8 +147,12 @@
     tokens = gathered.shape[0]
     me = lax.axis_index("row")
     arrived = gathered[...].astype(f32)
-    for slot, offset in enumerate(order):
-        owner = jnp.bitwise_xor(me, offset)
+    for slot, (table, shift, offset) in enumerate(order):
+        packed = sum(source << (2 * place) for place, source in enumerate(table))
+        high = lax.shift_right_logical(me, shift)
+        source = lax.shift_right_logical(jnp.int32(packed), 2 * high) & 3
+        low = jnp.bitwise_xor(me & ((1 << shift) - 1), offset)
+        owner = (source << shift) + low
         ordered[pl.ds(pl.multiple_of(owner * rows, rows), rows), :] = arrived[
             slot * rows : (slot + 1) * rows
         ]
@@ -170,12 +174,15 @@
     return max(d for d in range(1, rows + 1) if rows % d == 0 and (d == 1 or d * tokens <= 1024))
 
 
+SAME = (0, 1, 2, 3)
+QUARTERS = ((2, 3, 1, 0), (1, 0, 3, 2), (3, 2, 0, 1))
+
+
 def gather_rounds(count):
-    bits = count.bit_length() - 1
-    masks = [(1 << bit) | 1 for bit in range(bits - 1, 0, -1)] + [1]
-    if bits < 3:
-        return [[m] for m in masks]
-    return [[masks[0], masks[1], masks[0] ^ masks[1] ^ 1]] + [[m] for m in masks[2:]]
+    shift = count.bit_length() - 3
+    rounds = [[(q, 1 if shift else 0) for q in QUARTERS]]
+    rounds += [[(SAME, (1 << bit) | 1)] for bit in range(shift - 1, 0, -1)]
+    return shift, rounds + ([[(SAME, 1)]] if shift else [])
 
 
 def on_device(
@@ -237,14 +244,22 @@
     held_single, held_project, held_out = held[9:12]
     places = held[12:16]
 
-    order = [0]
+    shift, rounds = gather_rounds(count)
+    order = [(SAME, shift, 0)]
     gathered = single
     own = held_single
-    for step, masks in enumerate(gather_rounds(count)):
+    for step, moves in enumerate(rounds):
         parts = [own]
-        for mask in masks:
-            pairs = [(i, i ^ mask) for i in range(count)]
+        slots = list(order)
+        for targets, mask in moves:
+            pairs = [
+                (i, (targets[i >> shift] << shift) + ((i % (1 << shift)) ^ mask))
+                for i in range(count)
+            ]
             parts.append(lax.ppermute(gathered, "row", pairs))
+            for table, _, offset in order:
+                sources = table if targets == SAME else tuple(targets.index(q) for q in SAME)
+                slots.append((sources, shift, offset ^ mask))
         if step == 1:
             queries, gates, added, new_pair, parts[0] = pl.pallas_call(
                 functools.partial(late_kernel, chunk_of(late, tokens)),
@@ -274,7 +289,7 @@
                 late_pair,
                 own,
             )
-        order = order + [o ^ mask for mask in masks for o in order]
+        order = slots
         gathered = own = jnp.concatenate(parts, axis=0)
 
     update = pl.pallas_call(

time: 15.7 us -> 15.2 us (0.968)
  starting transfers between devices: 7.81 us -> 7.12 us
    ppermute x5, starting transfers between devices: 7.81 us -> 7.12 us  [on_device(): parts.append(lax.ppermute(gathered, 'row', pairs))]
  transfers between devices with their start and end apart: 5 -> 5, of which waited for: 4 -> 2; matrix products, arithmetic and copies ran while one was open for 0% -> 0% of each run, Pallas kernels for 27% -> 28%
where the time goes in v4:
time: 15.2 us; the launch traced here: 15 us
  starting transfers between devices  7.12 us (47%)
  Pallas kernels  5.74 us (38%)
  waiting for transfers between devices  1.41 us (9%)
  between operations  0.7 us (5%)
    ppermute x5, starting transfers between devices, on_device(): parts.append(lax.ppermute(gathered, 'row', pairs))  7.12 us
    pallas_call x1, Pallas kernels, on_device(): pl.pallas_call(functools.partial(early_kernel, early, chunk_of(early, tok...  2.81 us
    pallas_call x1, Pallas kernels, on_device(): pl.pallas_call(functools.partial(attend_kernel, order), out_shape=jax.Sha...  1.53 us
    ppermute x5, waiting for transfers between devices, on_device(): parts.append(lax.ppermute(gathered, 'row', pairs))  1.41 us
    pallas_call x1, Pallas kernels, on_device(): pl.pallas_call(functools.partial(late_kernel, chunk_of(late, tokens)), ou...  1.4 us
  transfers between devices with their start and end apart: 5, of which 2 were waited for; matrix products, arithmetic and copies ran while one was open for 0% of the time, Pallas kernels for 28%

profile of v4, /device:TPU:0, one launch (start us, length us, event | category | flops | bytes accessed | tf_op | source)
XLA Modules:
  0.0 15.0 jit_solution(6796642395439045367)
XLA Ops:
  0.6 3.5 %collective-permute-start = (bf16[8,384]{1,0:T(8,128)(2,1)}, bf16[8,384]{1,0:T(8,128)(2,1)S(1)}, u32[]{:S(2)}, u32[]{:S(2)}) collective-permute-start(bf16[8,384]{1,0:T(8,128)(2,1)} %refs_7_.1), channel_id=1, source_target_pairs={{0,9},{1,8},{2,11},{3,10},{4,13},{5,12},{6,15},{7,14},{8,5},{9,4},... | collective-permute-start | bytes 18440 | tf_op jit(solution)/shard_map/ppermute | solution.py:259
  4.2 1.1 %collective-permute-start.2 = (bf16[8,384]{1,0:T(8,128)(2,1)}, bf16[8,384]{1,0:T(8,128)(2,1)S(1)}, u32[]{:S(2)}, u32[]{:S(2)}) collective-permute-start(bf16[8,384]{1,0:T(8,128)(2,1)} %refs_7_.1), channel_id=1, source_target_pairs={{0,13},{1,12},{2,15},{3,14},{4,9},{5,8},{6,11},{7,10},{8,1},{9,0},... | collective-permute-start | bytes 18440 | tf_op jit(solution)/shard_map/ppermute | solution.py:259
  5.2 0.8 %collective-permute-start.1 = (bf16[8,384]{1,0:T(8,128)(2,1)}, bf16[8,384]{1,0:T(8,128)(2,1)S(1)}, u32[]{:S(2)}, u32[]{:S(2)}) collective-permute-start(bf16[8,384]{1,0:T(8,128)(2,1)} %refs_7_.1), channel_id=1, source_target_pairs={{0,5},{1,4},{2,7},{3,6},{4,1},{5,0},{6,3},{7,2},{8,13},{9,12},{10,... | collective-permute-start | bytes 18440 | tf_op jit(solution)/shard_map/ppermute | solution.py:259
  6.0 2.8 %early.1 = (bf16[6,128,128]{2,1,0:T(8,128)(2,1)S(1)}, bf16[6,16,128]{2,1,0:T(8,128)(2,1)S(1)}, bf16[2,128,128]{2,1,0:T(8,128)(2,1)S(1)}, f32[128]{0:T(128)S(1)},...) custom-call(bf16[8,128,128]{2,1,0:T(8,128)(2,1)} %refs_0_.1, ...), custom_call_target="tpu_custom_call" | custom-call | tf_op jit(solution)/shard_map/early/pallas_call | solution.py:225
  8.9 0.0 collective-permute-done
  8.9 0.0 collective-permute-done.1
  8.9 0.0 collective-permute-done.2
  8.9 1.5 %collective-permute-start.3 = (bf16[32,384]{1,0:T(8,128)(2,1)S(1)}, bf16[32,384]{1,0:T(8,128)(2,1)S(1)}, u32[]{:S(2)}, u32[]{:S(2)}) collective-permute-start(bf16[32,384]{1,0:T(8,128)(2,1)S(1)} %constant_dynamic-update-slice_fusion.refs_15_), channel_id=1, source_target_pairs={{0,3},{1,2},{2,1},{3,0},{4,7},{5,6},{6,5},{7,4},{8,11},{9,10},{10,... | collective-permute-start | bytes 73736 | tf_op jit(solution)/shard_map/ppermute | solution.py:259
  10.4 1.4 %late.1 = (bf16[128,384]{1,0:T(8,128)(2,1)S(1)}, f32[8,384]{1,0:T(8,128)S(1)}, f32[8,16,128]{2,1,0:T(8,128)S(1)}, bf16[8,128,128]{2,1,0:T(8,128)(2,1)}, bf16[32,384]{1,0:T(8,128)(2,1)S(1)}) custom-call(f32[128]{0:T(128)S(1)} %get-tuple-element.23.refs_0_, f32[128]{0:T(128)S(1)} %get-tuple-element.24.refs_1_, bf16[128,512]{1,0:T(8,128)(2,1)S(1)} %get-tuple-element.25.refs_2_, ...), custom_call_target="tpu_custom_call" | custom-call | tf_op jit(solution)/shard_map/late/pallas_call | solution.py:264
  11.8 0.4 %collective-permute-done.3 = bf16[32,384]{1,0:T(8,128)(2,1)S(1)} collective-permute-done((bf16[32,384]{1,0:T(8,128)(2,1)S(1)}, bf16[32,384]{1,0:T(8,128)(2,1)S(1)}, u32[]{:S(2)}, u32[]{:S(2)}) %collective-permute-start.3) | collective-permute-done | bytes 24608 | tf_op jit(solution)/shard_map/ppermute | solution.py:259
  12.2 0.3 %collective-permute-start.4 = (bf16[64,384]{1,0:T(8,128)(2,1)S(1)}, bf16[64,384]{1,0:T(8,128)(2,1)S(1)}, u32[]{:S(2)}, u32[]{:S(2)}) collective-permute-start(bf16[64,384]{1,0:T(8,128)(2,1)S(1)} %pad_maximum_fusion.1), channel_id=1, source_target_pairs={{0,1},{1,0},{2,3},{3,2},{4,5},{5,4},{6,7},{7,6},{8,9},{9,8},{10,11... | collective-permute-start | bytes 147464 | tf_op jit(solution)/shard_map/ppermute | solution.py:259
  12.5 1.0 %collective-permute-done.4 = bf16[64,384]{1,0:T(8,128)(2,1)S(1)} collective-permute-done((bf16[64,384]{1,0:T(8,128)(2,1)S(1)}, bf16[64,384]{1,0:T(8,128)(2,1)S(1)}, u32[]{:S(2)}, u32[]{:S(2)}) %collective-permute-start.4) | collective-permute-done | bytes 49184 | tf_op jit(solution)/shard_map/ppermute | solution.py:259
  13.5 1.5 %attend.1 = bf16[8,384]{1,0:T(8,128)(2,1)} custom-call(bf16[128,384]{1,0:T(8,128)(2,1)S(1)} %pad_maximum_fusion.gathered, bf16[384,1536]{1,0:T(8,128)(2,1)S(1)} %get-tuple-element.30.refs_7_.w_project, bf16[128,384]{1,0:T(8,128)(2,1)S(1)} %get-tuple-element.40.queries, f32[8,384]{1,0:T(8,128)S(1)} %get-tuple-element.41.gates, ...), custom_call_target="tpu_custom_call" | custom-call | tf_op jit(solution)/shard_map/attend/pallas_call | solution.py:295
  (6 shorter events, 0.0 us)
Async XLA Ops:
  0.6 8.2 %collective-permute-start = (bf16[8,384]{1,0:T(8,128)(2,1)}, bf16[8,384]{1,0:T(8,128)(2,1)S(1)}, u32[]{:S(2)}, u32[]{:S(2)}) collective-permute-start(bf16[8,384]{1,0:T(8,128)(2,1)} %refs_7_.1), channel_id=1, source_target_pairs={{0,9},{1,8},{2,11},{3,10},{4,13},{5,12},{6,15},{7,14},{8,5},{9,4},... | collective-permute-start | bytes 18440 | tf_op jit(solution)/shard_map/ppermute | solution.py:259
  4.2 4.7 %collective-permute-start.2 = (bf16[8,384]{1,0:T(8,128)(2,1)}, bf16[8,384]{1,0:T(8,128)(2,1)S(1)}, u32[]{:S(2)}, u32[]{:S(2)}) collective-permute-start(bf16[8,384]{1,0:T(8,128)(2,1)} %refs_7_.1), channel_id=1, source_target_pairs={{0,13},{1,12},{2,15},{3,14},{4,9},{5,8},{6,11},{7,10},{8,1},{9,0},... | collective-permute-start | bytes 18440 | tf_op jit(solution)/shard_map/ppermute | solution.py:259
  5.2 3.6 %collective-permute-start.1 = (bf16[8,384]{1,0:T(8,128)(2,1)}, bf16[8,384]{1,0:T(8,128)(2,1)S(1)}, u32[]{:S(2)}, u32[]{:S(2)}) collective-permute-start(bf16[8,384]{1,0:T(8,128)(2,1)} %refs_7_.1), channel_id=1, source_target_pairs={{0,5},{1,4},{2,7},{3,6},{4,1},{5,0},{6,3},{7,2},{8,13},{9,12},{10,... | collective-permute-start | bytes 18440 | tf_op jit(solution)/shard_map/ppermute | solution.py:259
  8.9 3.3 %collective-permute-start.3 = (bf16[32,384]{1,0:T(8,128)(2,1)S(1)}, bf16[32,384]{1,0:T(8,128)(2,1)S(1)}, u32[]{:S(2)}, u32[]{:S(2)}) collective-permute-start(bf16[32,384]{1,0:T(8,128)(2,1)S(1)} %constant_dynamic-update-slice_fusion.refs_15_), channel_id=1, source_target_pairs={{0,3},{1,2},{2,1},{3,0},{4,7},{5,6},{6,5},{7,4},{8,11},{9,10},{10,... | collective-permute-start | bytes 73736 | tf_op jit(solution)/shard_map/ppermute | solution.py:259
  12.2 1.2 %collective-permute-start.4 = (bf16[64,384]{1,0:T(8,128)(2,1)S(1)}, bf16[64,384]{1,0:T(8,128)(2,1)S(1)}, u32[]{:S(2)}, u32[]{:S(2)}) collective-permute-start(bf16[64,384]{1,0:T(8,128)(2,1)S(1)} %pad_maximum_fusion.1), channel_id=1, source_target_pairs={{0,1},{1,0},{2,3},{3,2},{4,5},{5,4},{6,7},{7,6},{8,9},{9,8},{10,11... | collective-permute-start | bytes 147464 | tf_op jit(solution)/shard_map/ppermute | solution.py:259

commit v5 on v4

--- a/solution.py
+++ b/solution.py
@@ -91,8 +91,8 @@
     weights = refs[:6]
     single, w_project, table, chain, residue, mask = refs[6:12]
     early_pair, early_bias, late_pair, received = refs[12:16]
-    queries, gates, added, new_pair, passed = refs[16:21]
-    late_new, late_bias, sems = refs[21:]
+    queries, gates, added, sums, new_pair, passed = refs[16:22]
+    late_new, late_bias, sems = refs[22:]
     early = early_pair.shape[0]
     late = late_pair.shape[0]
     first_copy = pltpu.make_async_copy(early_pair, new_pair.at[pl.ds(0, early)], sems.at[0])
@@ -111,6 +111,7 @@
     queries[...] = spread.reshape(rows * HEADS, WIDTH).astype(bf16)
     gate = dot(normed, w_project[:, 3 * WIDTH :]).astype(bf16).astype(f32)
     gates[...] = jax.nn.sigmoid(gate)
+    sums[...] = dot(jnp.ones_like(normed), w_project[:, WIDTH : 3 * WIDTH])
 
     first = lax.axis_index("row") * rows
     chain_j = chain[...][None, :]
@@ -141,30 +142,37 @@
 
 
 def attend_kernel(
-    order, gathered, w_project, queries, gates, added, w_out, update, ordered
+    order, known, new, w_project, sums, queries, gates, added, w_out, update, ordered
 ):
     rows = gates.shape[0]
-    tokens = gathered.shape[0]
+    tokens = ordered.shape[0]
     me = lax.axis_index("row")
-    arrived = gathered[...].astype(f32)
+    arrived = (known[...].astype(f32), new[...].astype(f32))
+    half = known.shape[0] // rows
     for slot, (table, shift, offset) in enumerate(order):
         packed = sum(source << (2 * place) for place, source in enumerate(table))
         high = lax.shift_right_logical(me, shift)
         source = lax.shift_right_logical(jnp.int32(packed), 2 * high) & 3
         low = jnp.bitwise_xor(me & ((1 << shift) - 1), offset)
         owner = (source << shift) + low
-        ordered[pl.ds(pl.multiple_of(owner * rows, rows), rows), :] = arrived[
-            slot * rows : (slot + 1) * rows
+        place = slot % half
+        ordered[pl.ds(pl.multiple_of(owner * rows, rows), rows), :] = arrived[slot // half][
+            place * rows : (place + 1) * rows
         ]
-    normed = layer_norm(ordered[...]).astype(bf16)
-    keys = dot(normed, w_project[:, WIDTH : 2 * WIDTH]).astype(bf16)
-    values = dot(normed, w_project[:, 2 * WIDTH : 3 * WIDTH]).astype(bf16)
+    single = ordered[...]
+    raw = dot(single.astype(bf16), w_project[:, WIDTH : 3 * WIDTH])
+    middle = jnp.mean(single, axis=-1, keepdims=True)
+    centred = single - middle
+    spread = jnp.mean(centred * centred, axis=-1, keepdims=True)
+    both = ((raw - middle * sums[0:1, :]) * lax.rsqrt(spread + EPSILON)).astype(bf16)
+    keys = both[:, :WIDTH]
+    values = both[:, WIDTH:]
     extra = added[...].reshape(rows * HEADS, tokens)
     scores = dot_nt(queries[...], keys) * (1.0 / math.sqrt(HEAD_DIM)) + extra
     scores = jnp.where(extra > -100000000.0, scores, MASKED)
     expons = jnp.exp(scores - jnp.max(scores, axis=1, keepdims=True))
     totals = jnp.sum(expons, axis=1, keepdims=True)
-    mixed = dot(expons.astype(bf16), values) / totals
+    mixed = dot(expons.astype(bf16), values) * (1.0 / totals)
     mixed = jnp.where(head_mask(rows), mixed.reshape(rows, HEADS, WIDTH), 0.0)
     gated = (gates[...] * jnp.sum(mixed, axis=1)).astype(bf16)
     update[...] = dot(gated, w_out[...]).astype(bf16)
@@ -261,17 +269,18 @@
                 sources = table if targets == SAME else tuple(targets.index(q) for q in SAME)
                 slots.append((sources, shift, offset ^ mask))
         if step == 1:
-            queries, gates, added, new_pair, parts[0] = pl.pallas_call(
+            queries, gates, added, sums, new_pair, parts[0] = pl.pallas_call(
                 functools.partial(late_kernel, chunk_of(late, tokens)),
                 out_shape=(
                     jax.ShapeDtypeStruct((rows * HEADS, width), bf16),
                     jax.ShapeDtypeStruct((rows, width), f32),
                     jax.ShapeDtypeStruct((rows, HEADS, tokens), f32),
+                    jax.ShapeDtypeStruct((rows, 2 * WIDTH), f32),
                     jax.ShapeDtypeStruct(pair.shape, bf16),
                     jax.ShapeDtypeStruct(own.shape, own.dtype),
                 ),
                 in_specs=[VMEM] * 16,
-                out_specs=(VMEM, VMEM, VMEM, ANY, VMEM),
+                out_specs=(VMEM, VMEM, VMEM, VMEM, ANY, VMEM),
                 scratch_shapes=[
                     pltpu.VMEM((late,) + pair.shape[1:], bf16),
                     pltpu.VMEM((late, HEADS, tokens), bf16),
@@ -295,12 +304,12 @@
     update = pl.pallas_call(
         functools.partial(attend_kernel, order),
         out_shape=jax.ShapeDtypeStruct((rows, width), bf16),
-        in_specs=[VMEM] * 6,
+        in_specs=[VMEM] * 8,
         out_specs=VMEM,
         scratch_shapes=[pltpu.VMEM((tokens, width), f32)],
         compiler_params=PARAMS,
         name="attend",
-    )(gathered, held_project, queries, gates, added, held_out)
+    )(*parts, held_project, sums, queries, gates, added, held_out)
     return (new_pair, update)
 
 

time: 15.2 us -> 15 us (0.987)
  waiting for transfers between devices: 1.41 us -> 1.17 us
    ppermute x5, waiting for transfers between devices: 1.41 us -> 1.17 us  [on_device(): parts.append(lax.ppermute(gathered, 'row', pairs))]
    pallas_call x1, Pallas kernels: 1.4 us -> 1.63 us  [on_device(): pl.pallas_call(functools.partial(late_kernel, chunk_of(late, tokens)), ou...]
  transfers between devices with their start and end apart: 5 -> 5, of which waited for: 2 -> 2; matrix products, arithmetic and copies ran while one was open for 0% -> 0% of each run, Pallas kernels for 28% -> 30%
where the time goes in v5:
time: 15 us; the launch traced here: 14.9 us
  starting transfers between devices  7.12 us (47%)
  Pallas kernels  5.86 us (39%)
  waiting for transfers between devices  1.17 us (8%)
  between operations  0.7 us (5%)
    ppermute x5, starting transfers between devices, on_device(): parts.append(lax.ppermute(gathered, 'row', pairs))  7.12 us
    pallas_call x1, Pallas kernels, on_device(): pl.pallas_call(functools.partial(early_kernel, early, chunk_of(early, tok...  2.81 us
    pallas_call x1, Pallas kernels, on_device(): pl.pallas_call(functools.partial(late_kernel, chunk_of(late, tokens)), ou...  1.63 us
    pallas_call x1, Pallas kernels, on_device(): pl.pallas_call(functools.partial(attend_kernel, order), out_shape=jax.Sha...  1.41 us
    ppermute x5, waiting for transfers between devices, on_device(): parts.append(lax.ppermute(gathered, 'row', pairs))  1.17 us
  transfers between devices with their start and end apart: 5, of which 2 were waited for; matrix products, arithmetic and copies ran while one was open for 0% of the time, Pallas kernels for 30%

profile of v5, /device:TPU:0, one launch (start us, length us, event | category | flops | bytes accessed | tf_op | source)
XLA Modules:
  0.0 14.9 jit_solution(1338568793926786868)
XLA Ops:
  0.6 3.5 %collective-permute-start = (bf16[8,384]{1,0:T(8,128)(2,1)}, bf16[8,384]{1,0:T(8,128)(2,1)S(1)}, u32[]{:S(2)}, u32[]{:S(2)}) collective-permute-start(bf16[8,384]{1,0:T(8,128)(2,1)} %refs_7_.1), channel_id=1, source_target_pairs={{0,9},{1,8},{2,11},{3,10},{4,13},{5,12},{6,15},{7,14},{8,5},{9,4},... | collective-permute-start | bytes 18440 | tf_op jit(solution)/shard_map/ppermute | solution.py:267
  4.2 1.1 %collective-permute-start.2 = (bf16[8,384]{1,0:T(8,128)(2,1)}, bf16[8,384]{1,0:T(8,128)(2,1)S(1)}, u32[]{:S(2)}, u32[]{:S(2)}) collective-permute-start(bf16[8,384]{1,0:T(8,128)(2,1)} %refs_7_.1), channel_id=1, source_target_pairs={{0,13},{1,12},{2,15},{3,14},{4,9},{5,8},{6,11},{7,10},{8,1},{9,0},... | collective-permute-start | bytes 18440 | tf_op jit(solution)/shard_map/ppermute | solution.py:267
  5.2 0.8 %collective-permute-start.1 = (bf16[8,384]{1,0:T(8,128)(2,1)}, bf16[8,384]{1,0:T(8,128)(2,1)S(1)}, u32[]{:S(2)}, u32[]{:S(2)}) collective-permute-start(bf16[8,384]{1,0:T(8,128)(2,1)} %refs_7_.1), channel_id=1, source_target_pairs={{0,5},{1,4},{2,7},{3,6},{4,1},{5,0},{6,3},{7,2},{8,13},{9,12},{10,... | collective-permute-start | bytes 18440 | tf_op jit(solution)/shard_map/ppermute | solution.py:267
  6.0 2.8 %early.1 = (bf16[6,128,128]{2,1,0:T(8,128)(2,1)S(1)}, bf16[6,16,128]{2,1,0:T(8,128)(2,1)S(1)}, bf16[2,128,128]{2,1,0:T(8,128)(2,1)S(1)}, f32[128]{0:T(128)S(1)},...) custom-call(bf16[8,128,128]{2,1,0:T(8,128)(2,1)} %refs_0_.1, ...), custom_call_target="tpu_custom_call" | custom-call | tf_op jit(solution)/shard_map/early/pallas_call | solution.py:233
  8.9 0.0 collective-permute-done
  8.9 0.0 collective-permute-done.1
  8.9 0.0 collective-permute-done.2
  8.9 1.5 %collective-permute-start.3 = (bf16[32,384]{1,0:T(8,128)(2,1)S(1)}, bf16[32,384]{1,0:T(8,128)(2,1)S(1)}, u32[]{:S(2)}, u32[]{:S(2)}) collective-permute-start(bf16[32,384]{1,0:T(8,128)(2,1)S(1)} %constant_dynamic-update-slice_fusion.refs_15_), channel_id=1, source_target_pairs={{0,3},{1,2},{2,1},{3,0},{4,7},{5,6},{6,5},{7,4},{8,11},{9,10},{10,... | collective-permute-start | bytes 73736 | tf_op jit(solution)/shard_map/ppermute | solution.py:267
  10.4 1.6 %late.1 = (bf16[128,384]{1,0:T(8,128)(2,1)S(1)}, f32[8,384]{1,0:T(8,128)S(1)}, f32[8,16,128]{2,1,0:T(8,128)S(1)}, f32[8,768]{1,0:T(8,128)S(1)}, bf16[8,128,128]{...) custom-call(f32[128]{0:T(128)S(1)} %get-tuple-element.24.refs_0_, f32[128]{0:T(128)S(1)} %get-tuple-element.25.refs_1_, ...), custom_call_target="tpu_custom_call" | custom-call | tf_op jit(solution)/shard_map/late/pallas_call | solution.py:272
  12.0 0.2 %collective-permute-done.3 = bf16[32,384]{1,0:T(8,128)(2,1)S(1)} collective-permute-done((bf16[32,384]{1,0:T(8,128)(2,1)S(1)}, bf16[32,384]{1,0:T(8,128)(2,1)S(1)}, u32[]{:S(2)}, u32[]{:S(2)}) %collective-permute-start.3) | collective-permute-done | bytes 24608 | tf_op jit(solution)/shard_map/ppermute | solution.py:267
  12.2 0.3 %collective-permute-start.4 = (bf16[64,384]{1,0:T(8,128)(2,1)S(1)}, bf16[64,384]{1,0:T(8,128)(2,1)S(1)}, u32[]{:S(2)}, u32[]{:S(2)}) collective-permute-start(bf16[64,384]{1,0:T(8,128)(2,1)S(1)} %constant_dynamic-update-slice_fusion.4.known), channel_id=1, source_target_pairs={{0,1},{1,0},{2,3},{3,2},{4,5},{5,4},{6,7},{7,6},{8,9},{9,8},{10,11... | collective-permute-start | bytes 147464 | tf_op jit(solution)/shard_map/ppermute | solution.py:267
  12.5 1.0 %collective-permute-done.4.new = bf16[64,384]{1,0:T(8,128)(2,1)S(1)} collective-permute-done((bf16[64,384]{1,0:T(8,128)(2,1)S(1)}, bf16[64,384]{1,0:T(8,128)(2,1)S(1)}, u32[]{:S(2)}, u32[]{:S(2)}) %collective-permute-start.4) | collective-permute-done | bytes 49184 | tf_op jit(solution)/shard_map/ppermute | solution.py:267
  13.5 1.4 %attend.1 = bf16[8,384]{1,0:T(8,128)(2,1)} custom-call(bf16[64,384]{1,0:T(8,128)(2,1)S(1)} %constant_dynamic-update-slice_fusion.4.known, bf16[64,384]{1,0:T(8,128)(2,1)S(1)} %collective-permute-done.4.new, bf16[384,1536]{1,0:T(8,128)(2,1)S(1)} %get-tuple-element.31.refs_7_.w_project, f32[8,768]{1,0:T(8,128)S(1)} %get-tuple-element.41.sums, ...), custom_call_target="tpu_custom_call" | custom-call | tf_op jit(solution)/shard_map/attend/pallas_call | solution.py:304
  (6 shorter events, 0.0 us)
Async XLA Ops:
  0.6 8.2 %collective-permute-start = (bf16[8,384]{1,0:T(8,128)(2,1)}, bf16[8,384]{1,0:T(8,128)(2,1)S(1)}, u32[]{:S(2)}, u32[]{:S(2)}) collective-permute-start(bf16[8,384]{1,0:T(8,128)(2,1)} %refs_7_.1), channel_id=1, source_target_pairs={{0,9},{1,8},{2,11},{3,10},{4,13},{5,12},{6,15},{7,14},{8,5},{9,4},... | collective-permute-start | bytes 18440 | tf_op jit(solution)/shard_map/ppermute | solution.py:267
  4.2 4.7 %collective-permute-start.2 = (bf16[8,384]{1,0:T(8,128)(2,1)}, bf16[8,384]{1,0:T(8,128)(2,1)S(1)}, u32[]{:S(2)}, u32[]{:S(2)}) collective-permute-start(bf16[8,384]{1,0:T(8,128)(2,1)} %refs_7_.1), channel_id=1, source_target_pairs={{0,13},{1,12},{2,15},{3,14},{4,9},{5,8},{6,11},{7,10},{8,1},{9,0},... | collective-permute-start | bytes 18440 | tf_op jit(solution)/shard_map/ppermute | solution.py:267
  5.2 3.6 %collective-permute-start.1 = (bf16[8,384]{1,0:T(8,128)(2,1)}, bf16[8,384]{1,0:T(8,128)(2,1)S(1)}, u32[]{:S(2)}, u32[]{:S(2)}) collective-permute-start(bf16[8,384]{1,0:T(8,128)(2,1)} %refs_7_.1), channel_id=1, source_target_pairs={{0,5},{1,4},{2,7},{3,6},{4,1},{5,0},{6,3},{7,2},{8,13},{9,12},{10,... | collective-permute-start | bytes 18440 | tf_op jit(solution)/shard_map/ppermute | solution.py:267
  8.9 3.3 %collective-permute-start.3 = (bf16[32,384]{1,0:T(8,128)(2,1)S(1)}, bf16[32,384]{1,0:T(8,128)(2,1)S(1)}, u32[]{:S(2)}, u32[]{:S(2)}) collective-permute-start(bf16[32,384]{1,0:T(8,128)(2,1)S(1)} %constant_dynamic-update-slice_fusion.refs_15_), channel_id=1, source_target_pairs={{0,3},{1,2},{2,1},{3,0},{4,7},{5,6},{6,5},{7,4},{8,11},{9,10},{10,... | collective-permute-start | bytes 73736 | tf_op jit(solution)/shard_map/ppermute | solution.py:267
  12.2 1.2 %collective-permute-start.4 = (bf16[64,384]{1,0:T(8,128)(2,1)S(1)}, bf16[64,384]{1,0:T(8,128)(2,1)S(1)}, u32[]{:S(2)}, u32[]{:S(2)}) collective-permute-start(bf16[64,384]{1,0:T(8,128)(2,1)S(1)} %constant_dynamic-update-slice_fusion.4.known), channel_id=1, source_target_pairs={{0,1},{1,0},{2,3},{3,2},{4,5},{5,4},{6,7},{7,6},{8,9},{9,8},{10,11... | collective-permute-start | bytes 147464 | tf_op jit(solution)/shard_map/ppermute | solution.py:267

commit v6 on v5

--- a/solution.py
+++ b/solution.py
@@ -15,7 +15,7 @@
 WIDTH = HEADS * HEAD_DIM
 EPSILON = 1e-05
 MASKED = -1000000000.0
-EARLY = 6
+EARLY = 5
 
 f32 = jnp.float32
 bf16 = jnp.bfloat16
@@ -91,8 +91,8 @@
     weights = refs[:6]
     single, w_project, table, chain, residue, mask = refs[6:12]
     early_pair, early_bias, late_pair, received = refs[12:16]
-    queries, gates, added, sums, new_pair, passed = refs[16:22]
-    late_new, late_bias, sems = refs[22:]
+    queries, gates, added, new_pair, passed = refs[16:21]
+    late_new, late_bias, sems = refs[21:]
     early = early_pair.shape[0]
     late = late_pair.shape[0]
     first_copy = pltpu.make_async_copy(early_pair, new_pair.at[pl.ds(0, early)], sems.at[0])
@@ -111,7 +111,6 @@
     queries[...] = spread.reshape(rows * HEADS, WIDTH).astype(bf16)
     gate = dot(normed, w_project[:, 3 * WIDTH :]).astype(bf16).astype(f32)
     gates[...] = jax.nn.sigmoid(gate)
-    sums[...] = dot(jnp.ones_like(normed), w_project[:, WIDTH : 3 * WIDTH])
 
     first = lax.axis_index("row") * rows
     chain_j = chain[...][None, :]
@@ -142,7 +141,7 @@
 
 
 def attend_kernel(
-    order, known, new, w_project, sums, queries, gates, added, w_out, update, ordered
+    order, known, new, w_project, queries, gates, added, w_out, update, ordered
 ):
     rows = gates.shape[0]
     tokens = ordered.shape[0]
@@ -160,11 +159,16 @@
             place * rows : (place + 1) * rows
         ]
     single = ordered[...]
-    raw = dot(single.astype(bf16), w_project[:, WIDTH : 3 * WIDTH])
+    ones = jnp.ones((16, WIDTH), bf16)
+    raw = dot(
+        jnp.concatenate([single.astype(bf16), ones], axis=0), w_project[:, WIDTH : 3 * WIDTH]
+    )
+    sums = raw[tokens : tokens + 1]
+    raw = raw[:tokens]
     middle = jnp.mean(single, axis=-1, keepdims=True)
     centred = single - middle
     spread = jnp.mean(centred * centred, axis=-1, keepdims=True)
-    both = ((raw - middle * sums[0:1, :]) * lax.rsqrt(spread + EPSILON)).astype(bf16)
+    both = ((raw - middle * sums) * lax.rsqrt(spread + EPSILON)).astype(bf16)
     keys = both[:, :WIDTH]
     values = both[:, WIDTH:]
     extra = added[...].reshape(rows * HEADS, tokens)
@@ -269,18 +273,17 @@
                 sources = table if targets == SAME else tuple(targets.index(q) for q in SAME)
                 slots.append((sources, shift, offset ^ mask))
         if step == 1:
-            queries, gates, added, sums, new_pair, parts[0] = pl.pallas_call(
+            queries, gates, added, new_pair, parts[0] = pl.pallas_call(
                 functools.partial(late_kernel, chunk_of(late, tokens)),
                 out_shape=(
                     jax.ShapeDtypeStruct((rows * HEADS, width), bf16),
                     jax.ShapeDtypeStruct((rows, width), f32),
                     jax.ShapeDtypeStruct((rows, HEADS, tokens), f32),
-                    jax.ShapeDtypeStruct((rows, 2 * WIDTH), f32),
                     jax.ShapeDtypeStruct(pair.shape, bf16),
                     jax.ShapeDtypeStruct(own.shape, own.dtype),
                 ),
                 in_specs=[VMEM] * 16,
-                out_specs=(VMEM, VMEM, VMEM, VMEM, ANY, VMEM),
+                out_specs=(VMEM, VMEM, VMEM, ANY, VMEM),
                 scratch_shapes=[
                     pltpu.VMEM((late,) + pair.shape[1:], bf16),
                     pltpu.VMEM((late, HEADS, tokens), bf16),
@@ -304,12 +307,12 @@
     update = pl.pallas_call(
         functools.partial(attend_kernel, order),
         out_shape=jax.ShapeDtypeStruct((rows, width), bf16),
-        in_specs=[VMEM] * 8,
+        in_specs=[VMEM] * 7,
         out_specs=VMEM,
         scratch_shapes=[pltpu.VMEM((tokens, width), f32)],
         compiler_params=PARAMS,
         name="attend",
-    )(*parts, held_project, sums, queries, gates, added, held_out)
+    )(*parts, held_project, queries, gates, added, held_out)
     return (new_pair, update)
 
 

time: 15 us -> 15.1 us (level)
  starting transfers between devices: 7.12 us -> 7.37 us
  waiting for transfers between devices: 1.17 us -> 0.96 us
    ppermute x5, starting transfers between devices: 7.12 us -> 7.37 us  [on_device(): parts.append(lax.ppermute(gathered, 'row', pairs))]
    ppermute x5, waiting for transfers between devices: 1.17 us -> 0.96 us  [on_device(): parts.append(lax.ppermute(gathered, 'row', pairs))]
    pallas_call x1, Pallas kernels: 2.81 us -> 2.64 us  [on_device(): pl.pallas_call(functools.partial(early_kernel, early, chunk_of(early, tok...]
  transfers between devices with their start and end apart: 5 -> 5, of which waited for: 2 -> 1; matrix products, arithmetic and copies ran while one was open for 0% -> 0% of each run, Pallas kernels for 30% -> 30%
where the time goes in v6:
time: 15.1 us; the launch traced here: 14.9 us
  starting transfers between devices  7.37 us (49%)
  Pallas kernels  5.84 us (39%)
  waiting for transfers between devices  0.96 us (6%)
  between operations  0.71 us (5%)
    ppermute x5, starting transfers between devices, on_device(): parts.append(lax.ppermute(gathered, 'row', pairs))  7.37 us
    pallas_call x1, Pallas kernels, on_device(): pl.pallas_call(functools.partial(early_kernel, early, chunk_of(early, tok...  2.64 us
    pallas_call x1, Pallas kernels, on_device(): pl.pallas_call(functools.partial(late_kernel, chunk_of(late, tokens)), ou...  1.77 us
    pallas_call x1, Pallas kernels, on_device(): pl.pallas_call(functools.partial(attend_kernel, order), out_shape=jax.Sha...  1.44 us
    ppermute x5, waiting for transfers between devices, on_device(): parts.append(lax.ppermute(gathered, 'row', pairs))  0.96 us
  transfers between devices with their start and end apart: 5, of which 1 were waited for; matrix products, arithmetic and copies ran while one was open for 0% of the time, Pallas kernels for 30%

profile of v6, /device:TPU:0, one launch (start us, length us, event | category | flops | bytes accessed | tf_op | source)
XLA Modules:
  0.0 14.9 jit_solution(3585201900084421121)
XLA Ops:
  0.6 3.5 %collective-permute-start = (bf16[8,384]{1,0:T(8,128)(2,1)}, bf16[8,384]{1,0:T(8,128)(2,1)S(1)}, u32[]{:S(2)}, u32[]{:S(2)}) collective-permute-start(bf16[8,384]{1,0:T(8,128)(2,1)} %refs_7_.1), channel_id=1, source_target_pairs={{0,9},{1,8},{2,11},{3,10},{4,13},{5,12},{6,15},{7,14},{8,5},{9,4},... | collective-permute-start | bytes 18440 | tf_op jit(solution)/shard_map/ppermute | solution.py:271
  4.2 1.1 %collective-permute-start.2 = (bf16[8,384]{1,0:T(8,128)(2,1)}, bf16[8,384]{1,0:T(8,128)(2,1)S(1)}, u32[]{:S(2)}, u32[]{:S(2)}) collective-permute-start(bf16[8,384]{1,0:T(8,128)(2,1)} %refs_7_.1), channel_id=1, source_target_pairs={{0,13},{1,12},{2,15},{3,14},{4,9},{5,8},{6,11},{7,10},{8,1},{9,0},... | collective-permute-start | bytes 18440 | tf_op jit(solution)/shard_map/ppermute | solution.py:271
  5.2 0.8 %collective-permute-start.1 = (bf16[8,384]{1,0:T(8,128)(2,1)}, bf16[8,384]{1,0:T(8,128)(2,1)S(1)}, u32[]{:S(2)}, u32[]{:S(2)}) collective-permute-start(bf16[8,384]{1,0:T(8,128)(2,1)} %refs_7_.1), channel_id=1, source_target_pairs={{0,5},{1,4},{2,7},{3,6},{4,1},{5,0},{6,3},{7,2},{8,13},{9,12},{10,... | collective-permute-start | bytes 18440 | tf_op jit(solution)/shard_map/ppermute | solution.py:271
  6.0 2.6 %early.1 = (bf16[5,128,128]{2,1,0:T(8,128)(2,1)S(1)}, bf16[5,16,128]{2,1,0:T(8,128)(2,1)S(1)}, bf16[3,128,128]{2,1,0:T(8,128)(2,1)S(1)}, f32[128]{0:T(128)S(1)},...) custom-call(bf16[8,128,128]{2,1,0:T(8,128)(2,1)} %refs_0_.1, ...), custom_call_target="tpu_custom_call" | custom-call | tf_op jit(solution)/shard_map/early/pallas_call | solution.py:237
  8.7 0.0 collective-permute-done
  8.7 0.0 collective-permute-done.1
  8.7 0.0 collective-permute-done.2
  8.8 1.6 %collective-permute-start.3 = (bf16[32,384]{1,0:T(8,128)(2,1)S(1)}, bf16[32,384]{1,0:T(8,128)(2,1)S(1)}, u32[]{:S(2)}, u32[]{:S(2)}) collective-permute-start(bf16[32,384]{1,0:T(8,128)(2,1)S(1)} %constant_dynamic-update-slice_fusion.refs_15_), channel_id=1, source_target_pairs={{0,3},{1,2},{2,1},{3,0},{4,7},{5,6},{6,5},{7,4},{8,11},{9,10},{10,... | collective-permute-start | bytes 73736 | tf_op jit(solution)/shard_map/ppermute | solution.py:271
  10.4 1.8 %late.1 = (bf16[128,384]{1,0:T(8,128)(2,1)S(1)}, f32[8,384]{1,0:T(8,128)S(1)}, f32[8,16,128]{2,1,0:T(8,128)S(1)}, bf16[8,128,128]{2,1,0:T(8,128)(2,1)}, bf16[32,384]{1,0:T(8,128)(2,1)S(1)}) custom-call(f32[128]{0:T(128)S(1)} %get-tuple-element.23.refs_0_, f32[128]{0:T(128)S(1)} %get-tuple-element.24.refs_1_, bf16[128,512]{1,0:T(8,128)(2,1)S(1)} %get-tuple-element.25.refs_2_, ...), custom_call_target="tpu_custom_call" | custom-call | tf_op jit(solution)/shard_map/late/pallas_call | solution.py:276
  12.2 0.0 collective-permute-done.3
  12.2 0.3 %collective-permute-start.4 = (bf16[64,384]{1,0:T(8,128)(2,1)S(1)}, bf16[64,384]{1,0:T(8,128)(2,1)S(1)}, u32[]{:S(2)}, u32[]{:S(2)}) collective-permute-start(bf16[64,384]{1,0:T(8,128)(2,1)S(1)} %constant_dynamic-update-slice_fusion.4.known), channel_id=1, source_target_pairs={{0,1},{1,0},{2,3},{3,2},{4,5},{5,4},{6,7},{7,6},{8,9},{9,8},{10,11... | collective-permute-start | bytes 147464 | tf_op jit(solution)/shard_map/ppermute | solution.py:271
  12.5 0.9 %collective-permute-done.4.new = bf16[64,384]{1,0:T(8,128)(2,1)S(1)} collective-permute-done((bf16[64,384]{1,0:T(8,128)(2,1)S(1)}, bf16[64,384]{1,0:T(8,128)(2,1)S(1)}, u32[]{:S(2)}, u32[]{:S(2)}) %collective-permute-start.4) | collective-permute-done | bytes 49184 | tf_op jit(solution)/shard_map/ppermute | solution.py:271
  13.5 1.4 %attend.1 = bf16[8,384]{1,0:T(8,128)(2,1)} custom-call(bf16[64,384]{1,0:T(8,128)(2,1)S(1)} %constant_dynamic-update-slice_fusion.4.known, bf16[64,384]{1,0:T(8,128)(2,1)S(1)} %collective-permute-done.4.new, bf16[384,1536]{1,0:T(8,128)(2,1)S(1)} %get-tuple-element.30.refs_7_.w_project, bf16[128,384]{1,0:T(8,128)(2,1)S(1)} %get-tuple-element.40.queries, ...), custom_call_target="tpu_custom_call" | custom-call | tf_op jit(solution)/shard_map/attend/pallas_call | solution.py:307
  (6 shorter events, 0.0 us)
Async XLA Ops:
  0.6 8.1 %collective-permute-start = (bf16[8,384]{1,0:T(8,128)(2,1)}, bf16[8,384]{1,0:T(8,128)(2,1)S(1)}, u32[]{:S(2)}, u32[]{:S(2)}) collective-permute-start(bf16[8,384]{1,0:T(8,128)(2,1)} %refs_7_.1), channel_id=1, source_target_pairs={{0,9},{1,8},{2,11},{3,10},{4,13},{5,12},{6,15},{7,14},{8,5},{9,4},... | collective-permute-start | bytes 18440 | tf_op jit(solution)/shard_map/ppermute | solution.py:271
  4.2 4.6 %collective-permute-start.2 = (bf16[8,384]{1,0:T(8,128)(2,1)}, bf16[8,384]{1,0:T(8,128)(2,1)S(1)}, u32[]{:S(2)}, u32[]{:S(2)}) collective-permute-start(bf16[8,384]{1,0:T(8,128)(2,1)} %refs_7_.1), channel_id=1, source_target_pairs={{0,13},{1,12},{2,15},{3,14},{4,9},{5,8},{6,11},{7,10},{8,1},{9,0},... | collective-permute-start | bytes 18440 | tf_op jit(solution)/shard_map/ppermute | solution.py:271
  5.2 3.5 %collective-permute-start.1 = (bf16[8,384]{1,0:T(8,128)(2,1)}, bf16[8,384]{1,0:T(8,128)(2,1)S(1)}, u32[]{:S(2)}, u32[]{:S(2)}) collective-permute-start(bf16[8,384]{1,0:T(8,128)(2,1)} %refs_7_.1), channel_id=1, source_target_pairs={{0,5},{1,4},{2,7},{3,6},{4,1},{5,0},{6,3},{7,2},{8,13},{9,12},{10,... | collective-permute-start | bytes 18440 | tf_op jit(solution)/shard_map/ppermute | solution.py:271
  8.8 3.4 %collective-permute-start.3 = (bf16[32,384]{1,0:T(8,128)(2,1)S(1)}, bf16[32,384]{1,0:T(8,128)(2,1)S(1)}, u32[]{:S(2)}, u32[]{:S(2)}) collective-permute-start(bf16[32,384]{1,0:T(8,128)(2,1)S(1)} %constant_dynamic-update-slice_fusion.refs_15_), channel_id=1, source_target_pairs={{0,3},{1,2},{2,1},{3,0},{4,7},{5,6},{6,5},{7,4},{8,11},{9,10},{10,... | collective-permute-start | bytes 73736 | tf_op jit(solution)/shard_map/ppermute | solution.py:271
  12.2 1.3 %collective-permute-start.4 = (bf16[64,384]{1,0:T(8,128)(2,1)S(1)}, bf16[64,384]{1,0:T(8,128)(2,1)S(1)}, u32[]{:S(2)}, u32[]{:S(2)}) collective-permute-start(bf16[64,384]{1,0:T(8,128)(2,1)S(1)} %constant_dynamic-update-slice_fusion.4.known), channel_id=1, source_target_pairs={{0,1},{1,0},{2,3},{3,2},{4,5},{5,4},{6,7},{7,6},{8,9},{9,8},{10,11... | collective-permute-start | bytes 147464 | tf_op jit(solution)/shard_map/ppermute | solution.py:271
